TPU v7x, 256 devices: a whole 4x4x8 slice. The times are simulated.
256 devices in a mesh: rows: 8 (over y, x_hi), blk: 16 (over z, x_lo), rep: 2 (over core).
Axes of the slice: x: 4 (x_hi: 2, x_lo: 2; x = x_hi * 2 + x_lo), y: 4, z: 8, core: 2. Of those that a mesh axis runs over, the one named last changes fastest.
Arguments:
- pair_left: bfloat16 [1024, 256, 128], P(('rep', 'rows'), 'blk'), parts along dimension 0, may hold values from -6 to 6
- pair_right: bfloat16 [1024, 256, 128], P(('rep', 'blk'), 'rows'), parts along dimension 0, may hold values from -6 to 6
- pair_middle: bfloat16 [1024, 512, 128], P(('rep', 'rows'), 'blk'), parts along dimension 0, may hold values from -6 to 6
- cotangent: bfloat16 [1024, 512, 128], P(('rep', 'rows'), 'blk'), parts along dimension 0, may hold values from -6 to 6
- left_weight: bfloat16 [128, 256], replicated, may hold values from -0.5 to 0.5
- right_weight: bfloat16 [128, 256], replicated, may hold values from -0.5 to 0.5
- gate_weight: bfloat16 [128, 128], replicated, may hold values from -0.5 to 0.5
- output_weight: bfloat16 [128, 128], replicated, may hold values from -0.5 to 0.5
Outputs:
- update: bfloat16 [1024, 512, 128], P(('rep', 'rows'), 'blk'), parts along dimension 0
- grad_left: bfloat16 [1024, 256, 128], P(('rep', 'rows'), 'blk'), parts along dimension 0
- grad_right: bfloat16 [1024, 256, 128], P(('rep', 'blk'), 'rows'), parts along dimension 0
- grad_middle: bfloat16 [1024, 512, 128], P(('rep', 'rows'), 'blk'), parts along dimension 0
- left_delta: float32 [256, 256], P('rep'), parts along dimension 0
- right_delta: float32 [256, 256], P('rep'), parts along dimension 0
- gate_delta: float32 [256, 128], P('rep'), parts along dimension 0
- output_delta: float32 [256, 128], P('rep'), parts along dimension 0
There are 2 independent parts, one for each index of `rep`. A program takes and returns all parts, laid end to end along the dimension named above; an argument that names none is the same for every part. Nothing has to cross between parts.
All inputs are finite; a program needn't handle non-finite values.
Results may differ from a plain program's by a relative error of at most 0.025.
Values may be sent and summed in bfloat16 or wider, within the bound.
A program may use at most 64 MiB of HBM per device.

v0:
```python
import jax
import jax.numpy as jnp
from jax import lax
from jax.sharding import PartitionSpec as P

epsilon = 1e-05


def normalize(field):
    values = field.astype(jnp.float32)
    centred = values - jnp.mean(values, axis=-1, keepdims=True)
    inverse = lax.rsqrt(jnp.mean(centred * centred, axis=-1, keepdims=True) + epsilon)
    return (centred * inverse, inverse)


def normalize_back(normed, inverse, upstream):
    first = jnp.mean(upstream, axis=-1, keepdims=True)
    second = jnp.mean(upstream * normed, axis=-1, keepdims=True)
    return inverse * (upstream - first - normed * second)


def flat_dot(inputs, weight):
    flat = inputs.reshape(-1, inputs.shape[-1])
    result = jnp.dot(flat, weight, preferred_element_type=jnp.float32)
    return result.reshape(inputs.shape[:-1] + (weight.shape[1],))


def outer_sum(inputs, grads):
    flat_in = inputs.reshape(-1, inputs.shape[-1])
    flat_back = grads.reshape(-1, grads.shape[-1])
    return jnp.einsum("rc,rd->cd", flat_in, flat_back, preferred_element_type=jnp.float32)


def gated_project(inputs, weight):
    width = weight.shape[1] // 2
    mixed_cols = flat_dot(inputs, weight)
    linear = mixed_cols[..., :width]
    switch = jax.nn.sigmoid(mixed_cols[..., width:])
    return (switch * linear, switch, linear)


def gated_back(inputs, switch, linear, upstream, weight):
    back_linear = upstream * switch
    back_gate = upstream * linear * switch * (1.0 - switch)
    joined = jnp.concatenate([back_linear, back_gate], axis=-1).astype(jnp.bfloat16)
    input_term = jnp.einsum("...d,cd->...c", joined, weight, preferred_element_type=jnp.float32)
    return (outer_sum(inputs, joined), input_term)


def per_device(
    pair_left,
    pair_right,
    pair_middle,
    cotangent,
    left_weight,
    right_weight,
    gate_weight,
    output_weight,
):
    left_norm, left_inverse = normalize(pair_left)
    left_input = left_norm.astype(jnp.bfloat16)
    left_act, left_switch, left_linear = gated_project(left_input, left_weight)
    left_slab = left_act.astype(jnp.bfloat16)
    right_norm, right_inverse = normalize(pair_right)
    right_input = right_norm.astype(jnp.bfloat16)
    right_act, right_switch, right_linear = gated_project(right_input, right_weight)
    right_slab = right_act.astype(jnp.bfloat16)
    right_whole = lax.all_gather(right_slab, "rows", axis=1, tiled=True)
    left_whole = lax.all_gather(left_slab, "blk", axis=1, tiled=True)
    triangle = jnp.einsum(
        "ikc,jkc->ijc", left_whole, right_whole, preferred_element_type=jnp.float32
    )
    tri_norm, tri_inverse = normalize(triangle)
    tri_input = tri_norm.astype(jnp.bfloat16)
    middle_norm, middle_inverse = normalize(pair_middle)
    middle_input = middle_norm.astype(jnp.bfloat16)
    gate = jax.nn.sigmoid(flat_dot(middle_input, gate_weight))
    head = flat_dot(tri_input, output_weight)
    update = (gate * head).astype(jnp.bfloat16)
    upstream = cotangent.astype(jnp.float32)
    head_back = (upstream * gate).astype(jnp.bfloat16)
    pre_back = (upstream * head * gate * (1.0 - gate)).astype(jnp.bfloat16)
    output_part = outer_sum(tri_input, head_back)
    gate_part = outer_sum(middle_input, pre_back)
    middle_up = jnp.einsum("ijd,cd->ijc", pre_back, gate_weight, preferred_element_type=jnp.float32)
    grad_middle = normalize_back(middle_norm, middle_inverse, middle_up).astype(jnp.bfloat16)
    tri_up = jnp.einsum("ijd,cd->ijc", head_back, output_weight, preferred_element_type=jnp.float32)
    tri_back = normalize_back(tri_norm, tri_inverse, tri_up).astype(jnp.bfloat16)
    partner = right_whole
    left_sums = lax.psum_scatter(
        jnp.einsum("ijc,jkc->kic", tri_back, partner, preferred_element_type=jnp.float32).astype(
            jnp.bfloat16
        ),
        "blk",
        scatter_dimension=0,
        tiled=True,
    ).astype(jnp.float32)
    left_back = jnp.transpose(left_sums, (1, 0, 2))
    partner = left_whole
    right_sums = lax.psum_scatter(
        jnp.einsum("ijc,ikc->kjc", tri_back, partner, preferred_element_type=jnp.float32).astype(
            jnp.bfloat16
        ),
        "rows",
        scatter_dimension=0,
        tiled=True,
    ).astype(jnp.float32)
    right_back = jnp.transpose(right_sums, (1, 0, 2))
    left_part, left_up = gated_back(left_input, left_switch, left_linear, left_back, left_weight)
    right_part, right_up = gated_back(
        right_input, right_switch, right_linear, right_back, right_weight
    )
    grad_left = normalize_back(left_norm, left_inverse, left_up).astype(jnp.bfloat16)
    grad_right = normalize_back(right_norm, right_inverse, right_up).astype(jnp.bfloat16)
    left_delta, right_delta, gate_delta, output_delta = lax.psum(
        (left_part, right_part, gate_part, output_part), ("rows", "blk")
    )
    return (
        update,
        grad_left,
        grad_right,
        grad_middle,
        left_delta,
        right_delta,
        gate_delta,
        output_delta,
    )


def solution(mesh):
    placed = (
        P(("rep", "rows"), "blk", None),
        P(("rep", "blk"), "rows", None),
        P(("rep", "rows"), "blk", None),
        P(("rep", "rows"), "blk", None),
        P(),
        P(),
        P(),
        P(),
    )
    return jax.shard_map(
        per_device,
        mesh=mesh,
        in_specs=placed,
        out_specs=(
            P(("rep", "rows"), "blk", None),
            P(("rep", "rows"), "blk", None),
            P(("rep", "blk"), "rows", None),
            P(("rep", "rows"), "blk", None),
            P("rep", None),
            P("rep", None),
            P("rep", None),
            P("rep", None),
        ),
        check_vma=False,
    )
```

profile of v0, /device:TPU:2, one launch (start us, length us, event | category | flops | bytes accessed | tf_op | source)
XLA Modules:
  0.0 647.7 jit_solution(9569078784805473505)
XLA Ops:
  7.2 1.2 convert_reduce_fusion.2
  8.5 1.4 fusion.38
  9.9 1.4 fusion.58
  17.2 1.4 fusion.4
  20.8 2.9 copy.79
  23.7 51.1 %all-gather.3.cloned.1.call-done = bf16[32,256,128]{2,1,0:T(8,128)(2,1)} async-done(((bf16[32,32,128]{2,1,0:T(8,128)(2,1)}), bf16[32,256,128]{2,1,0:T(8,128)(2,1)}) %all-gather.3.cloned.1.call-update) | async-done | bytes 2097168 | tf_op jit(solution)/shard_map/all_gather | solution.py:68
  74.8 3.4 copy.75
  78.2 117.8 %all-gather.5.cloned.1.call-done = bf16[64,256,128]{2,1,0:T(8,128)(2,1)} async-done(((bf16[64,16,128]{2,1,0:T(8,128)(2,1)}), bf16[64,256,128]{2,1,0:T(8,128)(2,1)}) %all-gather.5.cloned.1.call-update) | async-done | bytes 4194320 | tf_op jit(solution)/shard_map/all_gather | solution.py:69
  196.1 15.6 %copy.76 = bf16[64,256,128]{0,1,2:T(8,128)(2,1)} copy(bf16[64,256,128]{2,1,0:T(8,128)(2,1)} %all-gather.5.cloned.1.call-done) | data formatting | bytes 8388608 | tf_op jit(solution)/shard_map/all_gather | solution.py:69
  211.7 4.8 bitcast_reduce_fusion
  218.7 1.6 multiply_convert_fusion
  222.3 4.3 fusion.85
  226.6 4.5 copy.84
  231.4 4.5 fusion.84
  235.9 6.9 %copy.82 = bf16[128,256,64]{0,1,2:T(8,128)(2,1)} copy(bf16[128,256,64]{1,2,0:T(8,128)(2,1)} %fusion.84) | data formatting | bytes 8388608 | tf_op jit(solution)/shard_map/ijc,jkc->kic/dot_general | solution.py:91
  242.9 3.1 copy.77
  246.0 2.5 fusion.18
  249.3 2.7 fusion.80
  255.1 2.8 convolution_bitcast_fusion.3
  257.9 2.1 convolution_bitcast_fusion.2
  260.0 1.9 fusion.13
  262.0 49.1 %reduce-scatter.5.cloned.1.call-done = bf16[32,32,128]{2,0,1:T(8,128)(2,1)} async-done(((bf16[256,32,128]{2,0,1:T(8,128)(2,1)}), bf16[32,32,128]{2,0,1:T(8,128)(2,1)}) %reduce-scatter.5.cloned.1.call-update) | async-done | bytes 262160 | tf_op jit(solution)/shard_map/reduce_scatter | solution.py:100
  312.3 1.2 convolution_bitcast_fusion
  314.4 1.3 fusion.37
  315.7 96.0 %reduce-scatter.3.cloned.1.call-done = bf16[16,64,128]{2,0,1:T(8,128)(2,1)} async-done(((bf16[256,64,128]{2,0,1:T(8,128)(2,1)}), bf16[16,64,128]{2,0,1:T(8,128)(2,1)}) %reduce-scatter.3.cloned.1.call-update) | async-done | bytes 262160 | tf_op jit(solution)/shard_map/reduce_scatter | solution.py:90
  412.9 1.2 convolution_bitcast_fusion.1
  415.0 1.3 fusion.32
  416.4 218.7 %all-reduce.3.cloned.1.call-done = (f32[128,256]{1,0:T(8,128)}, f32[128,256]{1,0:T(8,128)}, f32[128,128]{1,0:T(8,128)}, f32[128,128]{1,0:T(8,128)}) async-done(((f32[128,256]{1,0:T(8,128)}, f32[128,256]{1,0:T(8,128)}, f32[128,128]{1,0:T(8,128)}, f32[128,128]{1,0:T(8,128)}), (f32[128,256]{1,0:T(8,128)}, f32[128,256]{1,0:T(8,128)}, f32[128,128]{1,0:T(8,128)}, ...) | async-done | bytes 393232 | tf_op jit(solution)/shard_map/psum | solution.py:115
  635.1 1.6 copy.94
  636.7 1.6 copy.95
  638.2 1.5 copy.96
  639.7 1.5 copy.97
  (116 shorter events, 20.4 us)
Async XLA Ops:
  7.2 2.7 copy-start
  7.2 6.0 copy-start.16
  7.2 67.6 %all-gather.3.cloned.1.call-start = ((), (), s32[]{:S(2)}) async-start(), calls=%async_computation.2 | async-start | bytes 2359296 | tf_op jit(solution)/shard_map/all_gather | solution.py:68
  8.4 5.4 copy-start.29
  9.9 3.6 copy-start.23
  13.1 2.1 copy-start.8
  13.1 182.9 %all-gather.5.cloned.1.call-start = ((), (), s32[]{:S(2)}) async-start(), calls=%async_computation.3 | async-start | bytes 4456448 | tf_op jit(solution)/shard_map/all_gather | solution.py:69
  13.8 1.8 copy-start.21
  13.8 3.4 copy-start.32
  15.2 295.9 %reduce-scatter.5.cloned.1.call-start = ((), (), s32[]{:S(2)}) async-start(), calls=%async_computation.5 | async-start | bytes 2359296 | tf_op jit(solution)/shard_map/reduce_scatter | solution.py:100
  17.2 2.4 copy-start.13
  17.2 2.4 copy-start.26
  218.1 4.1 copy-start.1
  231.2 180.6 %reduce-scatter.3.cloned.1.call-start = ((), (), s32[]{:S(2)}) async-start(), calls=%async_computation.4 | async-start | bytes 4456448 | tf_op jit(solution)/shard_map/reduce_scatter | solution.py:90
  242.8 3.2 copy-start.6
  242.8 392.3 %all-reduce.3.cloned.1.call-start = ((), (), s32[]{:S(2)}) async-start(), calls=%async_computation.6 | async-start | bytes 786432 | tf_op jit(solution)/shard_map/psum | solution.py:115
  242.9 6.4 copy-start.9
  246.0 6.0 copy-start.11
  246.0 3.3 copy-start.19
  246.0 3.3 copy-start.33
  255.1 2.8 copy-start.12
  255.1 4.9 copy-start.10
  255.1 4.9 copy-start.14
  255.1 4.9 copy-start.20
  255.1 4.9 copy-start.27
  255.1 4.9 copy-start.28
  257.9 53.2 %copy-start.4 = (f32[32,32,256]{2,1,0:T(8,128)S(1)}, f32[32,32,256]{2,1,0:T(8,128)}, u32[]{:S(2)}) copy-start(f32[32,32,256]{2,1,0:T(8,128)} %copy-done.3) | copy-start | bytes 3145732
  260.0 52.3 %copy-start.15 = (bf16[32,32,128]{2,1,0:T(8,128)(2,1)S(1)}, bf16[32,32,128]{2,1,0:T(8,128)(2,1)}, u32[]{:S(2)}) copy-start(bf16[32,32,128]{2,1,0:T(8,128)(2,1)} %param.9) | copy-start | bytes 786436
  260.0 52.3 %copy-start.24 = (f32[32,32]{1,0:T(8,128)S(1)}, f32[32,32]{1,0:T(8,128)}, u32[]{:S(2)}) copy-start(f32[32,32]{1,0:T(8,128)} %copy-done.23) | copy-start | bytes 12292
  311.1 2.5 copy-start.25
  313.5 99.4 %copy-start.22 = (f32[64,16]{1,0:T(8,128)S(1)}, f32[64,16]{1,0:T(8,128)}, u32[]{:S(2)}) copy-start(f32[64,16]{1,0:T(8,128)} %copy-done.21) | copy-start | bytes 12292
  314.4 99.8 %copy-start.30 = (bf16[128,256]{1,0:T(8,128)(2,1)S(1)}, bf16[128,256]{1,0:T(8,128)(2,1)}, u32[]{:S(2)}) copy-start(bf16[128,256]{1,0:T(8,128)(2,1)} %param.12) | copy-start | bytes 196612
  (7 other events, 6.7 us)
Sparse Core Ops, SparseCore 0:
  13.3 61.4 all-gather.2
  77.1 118.9 all-gather.4
  231.3 79.7 reduce-scatter.4
  313.5 98.2 reduce-scatter.2
  418.0 217.0 all-reduce.2
where the time goes:
time: 649 us; the launch traced here: 648 us
  waiting for transfers between devices  533 us (82%)
  local copies, waits for them, and re-layouts  53.3 us (8%)
  matrix products  31.5 us (5%)
  other arithmetic  15.3 us (2%)
  between operations  14.2 us (2%)
    psum x1, waiting for transfers between devices, per_device(): lax.psum((left_part, right_part, gate_part, output_part), ('rows', 'blk'))  219 us
    all_gather x1, waiting for transfers between devices, per_device(): left_whole = lax.all_gather(left_slab, 'blk', axis=1, tiled=True)  118 us
    reduce_scatter x1, waiting for transfers between devices, per_device(): lax.psum_scatter(jnp.einsum('ijc,jkc->kic', tri_back, partner, preferred_...  96 us
    all_gather x1, waiting for transfers between devices, per_device(): right_whole = lax.all_gather(right_slab, 'rows', axis=1, tiled=True)  51.1 us
    reduce_scatter x1, waiting for transfers between devices, per_device(): lax.psum_scatter(jnp.einsum('ijc,ikc->kjc', tri_back, partner, preferred_...  49.1 us
    all_gather x1, local copies, waits for them, and re-layouts, per_device(): left_whole = lax.all_gather(left_slab, 'blk', axis=1, tiled=True)  15.6 us
  transfers between devices with their start and end apart: 5, of which 5 were waited for; matrix products, arithmetic and copies ran while one was open for 7% of the time, Pallas kernels for 0%

commit v1 on v0

--- a/solution.py
+++ b/solution.py
@@ -1,6 +1,8 @@
 import jax
 import jax.numpy as jnp
 from jax import lax
+from jax.experimental import pallas as pl
+from jax.experimental.pallas import tpu as pltpu
 from jax.sharding import PartitionSpec as P
 
 epsilon = 1e-05
@@ -45,6 +47,75 @@
     joined = jnp.concatenate([back_linear, back_gate], axis=-1).astype(jnp.bfloat16)
     input_term = jnp.einsum("...d,cd->...c", joined, weight, preferred_element_type=jnp.float32)
     return (outer_sum(inputs, joined), input_term)
+
+
+def partner(index):
+    return {"rows": index // 16, "blk": lax.rem(index, 16)}
+
+
+def reduce_kernel(x_ref, o_ref, recv, total, sems):
+    me = lax.axis_index("rows") * 16 + lax.axis_index("blk")
+    barrier = pltpu.get_barrier_semaphore()
+
+    def greet(o, c):
+        p = lax.rem(me + o, 128)
+        pl.semaphore_signal(barrier, inc=1, device_id=partner(p), device_id_type=pl.DeviceIdType.MESH)
+        return c
+
+    lax.fori_loop(1, 128, greet, 0)
+    pl.semaphore_wait(barrier, 127)
+
+    def scatter(o, c):
+        p = lax.rem(me + o, 128)
+        pltpu.make_async_remote_copy(
+            src_ref=x_ref.at[p], dst_ref=recv.at[me], send_sem=sems.at[0], recv_sem=sems.at[1],
+            device_id=partner(p), device_id_type=pl.DeviceIdType.MESH).start()
+        return c
+
+    lax.fori_loop(1, 128, scatter, 0)
+    recv[pl.ds(me, 1)] = x_ref[pl.ds(me, 1)]
+    done = pltpu.make_async_remote_copy(
+        src_ref=x_ref.at[pl.ds(0, 127)], dst_ref=recv.at[pl.ds(0, 127)], send_sem=sems.at[0], recv_sem=sems.at[1],
+        device_id=partner(lax.rem(me + 1, 128)), device_id_type=pl.DeviceIdType.MESH)
+    done.wait_recv()
+    done.wait_send()
+    total[...] = jnp.sum(recv[...], axis=0)
+
+    def spread(o, c):
+        p = lax.rem(me + o, 128)
+        pltpu.make_async_remote_copy(
+            src_ref=total, dst_ref=o_ref.at[me], send_sem=sems.at[2], recv_sem=sems.at[3],
+            device_id=partner(p), device_id_type=pl.DeviceIdType.MESH).start()
+        return c
+
+    lax.fori_loop(1, 128, spread, 0)
+    o_ref[pl.ds(me, 1)] = total[...][None]
+    done = pltpu.make_async_remote_copy(
+        src_ref=x_ref.at[pl.ds(0, 127)], dst_ref=o_ref.at[pl.ds(0, 127)], send_sem=sems.at[2], recv_sem=sems.at[3],
+        device_id=partner(lax.rem(me + 1, 128)), device_id_type=pl.DeviceIdType.MESH)
+    done.wait_recv()
+    done.wait_send()
+
+
+def reduce_all(parts):
+    flat = jnp.concatenate([p.reshape(-1) for p in parts]).reshape(128, -1, 128)
+    total = pl.pallas_call(
+        reduce_kernel,
+        out_shape=jax.ShapeDtypeStruct(flat.shape, jnp.float32),
+        in_specs=[pl.BlockSpec(memory_space=pltpu.VMEM)],
+        out_specs=pl.BlockSpec(memory_space=pltpu.VMEM),
+        scratch_shapes=[
+            pltpu.VMEM(flat.shape, jnp.float32),
+            pltpu.VMEM(flat.shape[1:], jnp.float32),
+            pltpu.SemaphoreType.DMA((4,)),
+        ],
+        compiler_params=pltpu.CompilerParams(collective_id=0, has_side_effects=True),
+    )(flat).reshape(-1)
+    out, at = [], 0
+    for p in parts:
+        out.append(total[at:at + p.size].reshape(p.shape))
+        at += p.size
+    return out
 
 
 def per_device(
@@ -112,8 +183,8 @@
     )
     grad_left = normalize_back(left_norm, left_inverse, left_up).astype(jnp.bfloat16)
     grad_right = normalize_back(right_norm, right_inverse, right_up).astype(jnp.bfloat16)
-    left_delta, right_delta, gate_delta, output_delta = lax.psum(
-        (left_part, right_part, gate_part, output_part), ("rows", "blk")
+    left_delta, right_delta, gate_delta, output_delta = reduce_all(
+        (left_part, right_part, gate_part, output_part)
     )
     return (
         update,

time: 649 us -> 463 us (0.71)
  waiting for transfers between devices: 533 us -> 315 us
  Pallas kernels: 0 us -> 34.8 us
    psum x1 -> x0, waiting for transfers between devices: 219 us -> none  [per_device(): lax.psum((left_part, right_part, gate_part, output_part), ('rows', 'blk'))]
    pallas_call x0 -> x1, Pallas kernels: none -> 34.8 us  [reduce_all(): pl.pallas_call(reduce_kernel, out_shape=jax.ShapeDtypeStruct(flat.shape,...]
  transfers between devices with their start and end apart: 5 -> 4, of which waited for: 5 -> 4; matrix products, arithmetic and copies ran while one was open for 7% -> 10% of each run, Pallas kernels for 0% -> 0%
where the time goes in v1:
time: 463 us; the launch traced here: 462 us
  waiting for transfers between devices  315 us (68%)
  local copies, waits for them, and re-layouts  51.9 us (11%)
  Pallas kernels  34.8 us (8%)
  matrix products  30.3 us (7%)
  other arithmetic  15.3 us (3%)
  between operations  14.3 us (3%)
    all_gather x1, waiting for transfers between devices, per_device(): left_whole = lax.all_gather(left_slab, 'blk', axis=1, tiled=True)  118 us
    reduce_scatter x1, waiting for transfers between devices, per_device(): lax.psum_scatter(jnp.einsum('ijc,jkc->kic', tri_back, partner, preferred_...  96.6 us
    all_gather x1, waiting for transfers between devices, per_device(): right_whole = lax.all_gather(right_slab, 'rows', axis=1, tiled=True)  51.1 us
    reduce_scatter x1, waiting for transfers between devices, per_device(): lax.psum_scatter(jnp.einsum('ijc,ikc->kjc', tri_back, partner, preferred_...  49.1 us
    pallas_call x1, Pallas kernels, reduce_all(): pl.pallas_call(reduce_kernel, out_shape=jax.ShapeDtypeStruct(flat.shape,...  34.8 us
    all_gather x1, local copies, waits for them, and re-layouts, per_device(): left_whole = lax.all_gather(left_slab, 'blk', axis=1, tiled=True)  15.7 us
  transfers between devices with their start and end apart: 4, of which 4 were waited for; matrix products, arithmetic and copies ran while one was open for 10% of the time, Pallas kernels for 0%

profile of v1, /device:TPU:2, one launch (start us, length us, event | category | flops | bytes accessed | tf_op | source)
XLA Modules:
  0.0 461.7 jit_solution(4173567989590703379)
XLA Ops:
  7.2 1.2 convert_reduce_fusion.2
  8.5 1.4 fusion.38
  9.9 1.4 fusion.58
  11.3 1.0 copy-done.3
  17.2 1.4 fusion.4
  20.8 2.9 copy.93
  23.8 51.1 %all-gather.3.cloned.1.call-done = bf16[32,256,128]{2,1,0:T(8,128)(2,1)} async-done(((bf16[32,32,128]{2,1,0:T(8,128)(2,1)}), bf16[32,256,128]{2,1,0:T(8,128)(2,1)}) %all-gather.3.cloned.1.call-update) | async-done | bytes 2097168 | tf_op jit(solution)/shard_map/all_gather | solution.py:139
  74.8 3.4 copy.89
  78.2 117.8 %all-gather.5.cloned.1.call-done = bf16[64,256,128]{2,1,0:T(8,128)(2,1)} async-done(((bf16[64,16,128]{2,1,0:T(8,128)(2,1)}), bf16[64,256,128]{2,1,0:T(8,128)(2,1)}) %all-gather.5.cloned.1.call-update) | async-done | bytes 4194320 | tf_op jit(solution)/shard_map/all_gather | solution.py:140
  196.1 15.7 %copy.90 = bf16[64,256,128]{0,1,2:T(8,128)(2,1)} copy(bf16[64,256,128]{2,1,0:T(8,128)(2,1)} %all-gather.5.cloned.1.call-done) | data formatting | bytes 8388608 | tf_op jit(solution)/shard_map/all_gather | solution.py:140
  211.7 4.8 %bitcast_reduce_fusion = (f32[64,32]{0,1:T(8,128)S(1)}, f32[128,32,64]{2,1,0:T(8,128)S(1)}) fusion(bf16[32,256,128]{1,0,2:T(8,128)(2,1)S(1)} %copy.89, bf16[64,256,128]{0,1,2:T(8,128)(2,1)} %copy.90), kind=kOutput, calls=%fused_computation.4 | convolution fusion | flops 134477824 | bytes 7348224 | tf_op jit(solution)/shard_map/ikc,jkc->ijc/dot_general | solution.py:141
  218.7 1.6 multiply_convert_fusion
  221.3 1.0 copy-done.1
  222.3 4.3 fusion.87
  226.6 4.5 copy.98
  231.4 4.5 fusion.86
  235.9 6.9 %copy.96 = bf16[128,256,64]{0,1,2:T(8,128)(2,1)} copy(bf16[128,256,64]{1,2,0:T(8,128)(2,1)} %fusion.86) | data formatting | bytes 8388608 | tf_op jit(solution)/shard_map/ijc,jkc->kic/dot_general | solution.py:162
  242.9 3.1 copy.91
  246.0 2.5 fusion.18
  249.3 2.7 fusion.80
  255.1 2.8 convolution_bitcast_fusion.1
  257.9 2.1 convolution_bitcast_fusion
  260.0 1.9 fusion.13
  262.0 49.1 %reduce-scatter.5.cloned.1.call-done = bf16[32,32,128]{2,0,1:T(8,128)(2,1)} async-done(((bf16[256,32,128]{2,0,1:T(8,128)(2,1)}), bf16[32,32,128]{2,0,1:T(8,128)(2,1)}) %reduce-scatter.5.cloned.1.call-update) | async-done | bytes 262160 | tf_op jit(solution)/shard_map/reduce_scatter | solution.py:171
  311.1 1.2 fusion.45
  313.8 1.3 fusion.37
  315.2 96.6 %reduce-scatter.3.cloned.1.call-done = bf16[16,64,128]{2,0,1:T(8,128)(2,1)} async-done(((bf16[256,64,128]{2,0,1:T(8,128)(2,1)}), bf16[16,64,128]{2,0,1:T(8,128)(2,1)}) %reduce-scatter.3.cloned.1.call-update) | async-done | bytes 262160 | tf_op jit(solution)/shard_map/reduce_scatter | solution.py:161
  411.7 1.2 fusion.49
  415.4 34.8 %shard_map.143 = f32[128,6,128]{2,1,0:T(8,128)} custom-call(f32[128,6,128]{2,1,0:T(8,128)} %reshape.152.x_ref), custom_call_target="tpu_custom_call" | custom-call | tf_op jit(solution)/shard_map/pallas_call | solution.py:102
  450.2 1.1 slice.39
  451.3 1.2 slice.36
  453.8 1.3 fusion.32
  (120 shorter events, 19.7 us)
Async XLA Ops:
  7.2 2.7 copy-start
  7.2 6.0 %copy-start.16 = (bf16[64,16,128]{2,1,0:T(8,128)(2,1)S(1)}, bf16[64,16,128]{2,1,0:T(8,128)(2,1)}, u32[]{:S(2)}) copy-start(bf16[64,16,128]{2,1,0:T(8,128)(2,1)} %param.8) | copy-start | bytes 786436
  7.2 67.6 %all-gather.3.cloned.1.call-start = ((), (), s32[]{:S(2)}) async-start(), calls=%async_computation.2 | async-start | bytes 2359296 | tf_op jit(solution)/shard_map/all_gather | solution.py:139
  8.4 5.4 %copy-start.29 = (bf16[128,256]{1,0:T(8,128)(2,1)S(1)}, bf16[128,256]{1,0:T(8,128)(2,1)}, u32[]{:S(2)}) copy-start(bf16[128,256]{1,0:T(8,128)(2,1)} %param.12) | copy-start | bytes 196612
  9.9 3.6 copy-start.24
  13.1 2.1 copy-start.8
  13.2 182.9 %all-gather.5.cloned.1.call-start = ((), (), s32[]{:S(2)}) async-start(), calls=%async_computation.3 | async-start | bytes 4456448 | tf_op jit(solution)/shard_map/all_gather | solution.py:140
  13.8 1.8 copy-start.21
  13.9 3.4 copy-start.33
  15.2 295.9 %reduce-scatter.5.cloned.1.call-start = ((), (), s32[]{:S(2)}) async-start(), calls=%async_computation.5 | async-start | bytes 2359296 | tf_op jit(solution)/shard_map/reduce_scatter | solution.py:171
  17.2 2.4 copy-start.13
  17.2 2.4 copy-start.26
  216.6 1.6 copy-start.2
  218.2 4.1 copy-start.1
  231.2 180.5 %reduce-scatter.3.cloned.1.call-start = ((), (), s32[]{:S(2)}) async-start(), calls=%async_computation.4 | async-start | bytes 4456448 | tf_op jit(solution)/shard_map/reduce_scatter | solution.py:161
  242.8 3.1 copy-start.6
  242.8 6.4 %copy-start.9 = (bf16[64,32,128]{2,1,0:T(8,128)(2,1)S(1)}, bf16[64,32,128]{2,1,0:T(8,128)(2,1)}, u32[]{:S(2)}) copy-start(bf16[64,32,128]{2,1,0:T(8,128)(2,1)} %param.10) | copy-start | bytes 1572868
  246.0 6.0 %copy-start.11 = (bf16[64,32,128]{2,1,0:T(8,128)(2,1)}, bf16[64,32,128]{2,1,0:T(8,128)(2,1)S(1)}, u32[]{:S(2)}) copy-start(bf16[64,32,128]{2,1,0:T(8,128)(2,1)S(1)} %copy.91) | copy-start | bytes 1572868
  246.0 3.3 copy-start.19
  246.0 3.3 copy-start.34
  255.1 2.8 copy-start.12
  255.1 4.9 %copy-start.10 = (bf16[64,32,128]{2,1,0:T(8,128)(2,1)S(1)}, bf16[64,32,128]{2,1,0:T(8,128)(2,1)}, u32[]{:S(2)}) copy-start(bf16[64,32,128]{2,1,0:T(8,128)(2,1)} %param.10) | copy-start | bytes 1572868
  255.1 4.9 %copy-start.14 = (f32[64,32,128]{2,1,0:T(8,128)S(1)}, f32[64,32,128]{2,1,0:T(8,128)}, u32[]{:S(2)}) copy-start(f32[64,32,128]{2,1,0:T(8,128)} %get-tuple-element.32) | copy-start | bytes 3145732
  255.1 4.9 %copy-start.20 = (f32[64,32]{1,0:T(8,128)S(1)}, f32[64,32]{1,0:T(8,128)}, u32[]{:S(2)}) copy-start(f32[64,32]{1,0:T(8,128)} %copy-done.18) | copy-start | bytes 24580
  255.1 4.9 %copy-start.27 = (f32[64,32]{1,0:T(8,128)S(1)}, f32[64,32]{1,0:T(8,128)}, u32[]{:S(2)}) copy-start(f32[64,32]{1,0:T(8,128)} %copy.100) | copy-start | bytes 24580
  255.1 4.9 %copy-start.28 = (f32[64,32]{1,0:T(8,128)S(1)}, f32[64,32]{1,0:T(8,128)}, u32[]{:S(2)}) copy-start(f32[64,32]{1,0:T(8,128)} %copy.102) | copy-start | bytes 24580
  257.9 53.2 %copy-start.4 = (f32[32,32,256]{2,1,0:T(8,128)S(1)}, f32[32,32,256]{2,1,0:T(8,128)}, u32[]{:S(2)}) copy-start(f32[32,32,256]{2,1,0:T(8,128)} %copy-done.3) | copy-start | bytes 3145732
  260.0 52.3 %copy-start.15 = (bf16[32,32,128]{2,1,0:T(8,128)(2,1)S(1)}, bf16[32,32,128]{2,1,0:T(8,128)(2,1)}, u32[]{:S(2)}) copy-start(bf16[32,32,128]{2,1,0:T(8,128)(2,1)} %param.9) | copy-start | bytes 786436
  260.0 52.3 %copy-start.25 = (f32[32,32]{1,0:T(8,128)S(1)}, f32[32,32]{1,0:T(8,128)}, u32[]{:S(2)}) copy-start(f32[32,32]{1,0:T(8,128)} %copy-done.24) | copy-start | bytes 12292
  313.0 100.0 %copy-start.22 = (f32[64,16]{1,0:T(8,128)S(1)}, f32[64,16]{1,0:T(8,128)}, u32[]{:S(2)}) copy-start(f32[64,16]{1,0:T(8,128)} %copy-done.21) | copy-start | bytes 12292
  313.8 99.7 %copy-start.30 = (bf16[128,256]{1,0:T(8,128)(2,1)S(1)}, bf16[128,256]{1,0:T(8,128)(2,1)}, u32[]{:S(2)}) copy-start(bf16[128,256]{1,0:T(8,128)(2,1)} %param.12) | copy-start | bytes 196612
  412.9 1.6 copy-start.23
  (7 other events, 6.7 us)
Sparse Core Ops, SparseCore 0:
  13.3 61.4 all-gather.2
  77.1 118.9 all-gather.4
  231.3 79.7 reduce-scatter.4
  313.5 98.2 reduce-scatter.2

commit v2 on v0

v2 whole, which is shorter than its diff:
```python
import jax
import jax.numpy as jnp
from jax import lax
from jax.experimental import pallas as pl
from jax.experimental.pallas import tpu as pltpu
from jax.sharding import PartitionSpec as P

epsilon = 1e-05
F32 = jnp.float32
BF16 = jnp.bfloat16
MESH = pl.DeviceIdType.MESH
N = 128


def partner(p):
    return {"rows": p // 16, "blk": lax.rem(p, 16)}


def rows_norm(x):
    centred = x - jnp.mean(x, axis=-1, keepdims=True)
    inverse = lax.rsqrt(jnp.mean(centred * centred, axis=-1, keepdims=True) + epsilon)
    return centred * inverse, inverse


def rows_back(normed, inverse, up):
    first = jnp.mean(up, axis=-1, keepdims=True)
    second = jnp.mean(up * normed, axis=-1, keepdims=True)
    return inverse * (up - first - normed * second)


def dot(a, b, ca, cb):
    return lax.dot_general(a, b, (((ca,), (cb,)), ((), ())), preferred_element_type=F32)


def swap2(a, b):
    low = lax.broadcasted_iota(jnp.int32, a.shape, 1) < 64
    return (
        jnp.where(low, a, pltpu.roll(b, 64, 1)),
        jnp.where(low, pltpu.roll(a, 64, 1), b),
    )


def swap4(xs):
    y0, y2 = swap2(xs[0], xs[2])
    y1, y3 = swap2(xs[1], xs[3])
    low = (lax.broadcasted_iota(jnp.int32, y0.shape, 1) & 32) == 0
    outs = []
    for a, b in ((y0, y1), (y2, y3)):
        outs.append(jnp.where(low, a, pltpu.roll(b, 32, 1)))
        outs.append(jnp.where(low, pltpu.roll(a, 96, 1), b))
    return outs


def rows_at(start, size, step):
    return pl.ds(pl.multiple_of(start, step), size)


def kernel(
    left_ref, right_ref, mid_ref, cot_ref, lw_ref, rw_ref, gw_ref, ow_ref,
    update_ref, gleft_ref, gright_ref, gmid_ref, dleft_ref, dright_ref, dgate_ref, dout_ref,
    wide, send_a, send_b, send_c, send_d, recv_a, recv_b, recv_c, recv_d,
    norm_l, norm_r, inv_l, inv_r, in_l, in_r, lin, sw,
    lwt, rwt, mid_norm, mid_inv, mid_t, gate, head_back, tri_in, tri_t,
    lt, rt, tri, tb, lb, rb,
    sums, late_sums, early_recv, late_recv, early_total, late_total, early_all, late_all,
    sems,
):
    me = lax.axis_index("rows") * 16 + lax.axis_index("blk")
    barrier = pltpu.get_barrier_semaphore()

    def copy(src, dst, k, p):
        return pltpu.make_async_remote_copy(
            src_ref=src, dst_ref=dst, send_sem=sems.at[2 * k], recv_sem=sems.at[2 * k + 1],
            device_id=partner(p), device_id_type=MESH)

    def greet(o, c):
        pl.semaphore_signal(
            barrier, inc=1, device_id=partner(lax.rem(me + o, N)), device_id_type=MESH)
        return c

    lax.fori_loop(1, N, greet, 0)

    def spread(send, recv, k):
        def step(o, c):
            p = lax.rem(me + o, N)
            send[p] = wide[rows_at(p * 16, 16, 16), :].astype(BF16)
            copy(send.at[p], recv.at[me], k, p).start()
            return c
        lax.fori_loop(1, N, step, 0)
        recv[me] = wide[rows_at(me * 16, 16, 16), :].astype(BF16)

    def batch(send, recv, k):
        return copy(send.at[pl.ds(0, N - 1)], recv.at[pl.ds(0, N - 1)], k, lax.rem(me + 1, N))

    def widen(recv):
        def step(t, c):
            wide[rows_at(t * 256, 256, 256), :] = (
                recv[rows_at(t * 16, 16, 16)].astype(F32).reshape(256, 128))
            return c
        lax.fori_loop(0, 8, step, 0)

    lwt[...] = lw_ref[...].astype(F32).T.astype(BF16)
    rwt[...] = rw_ref[...].astype(F32).T.astype(BF16)

    def norm_step(t, c):
        at = rows_at(t * 128, 128, 128)
        for ref, normed, inverse in ((left_ref, norm_l, inv_l), (right_ref, norm_r, inv_r)):
            n, i = rows_norm(ref[at, :].astype(F32))
            normed[at, :] = n
            inverse[at, :] = jnp.broadcast_to(i, n.shape)
        return c

    lax.fori_loop(0, 8, norm_step, 0)

    def chunk(ref, q, side):
        if side == 0:
            return jnp.concatenate([ref[pl.ds(q + 8 * h, 64, stride=16), :] for h in range(2)], axis=0)
        return jnp.concatenate([ref[pl.ds(q + 8 * h, 32, stride=32), :] for h in range(4)], axis=0)

    def project(q, c):
        for side, (normed, inputs, wt) in enumerate(((norm_l, in_l, lwt), (norm_r, in_r, rwt))):
            x = chunk(normed, q, side).astype(BF16)
            inputs[q] = x
            pre = dot(wt[...], x, 1, 1)
            linear, switch = pre[:N], jax.nn.sigmoid(pre[N:])
            lin[side * 8 + q] = linear
            sw[side * 8 + q] = switch
            wide[pl.ds(side * 8 + q, N, stride=16), :] = linear * switch
        return c

    lax.fori_loop(0, 8, project, 0)

    pl.semaphore_wait(barrier, N - 1)
    spread(send_a, recv_a, 0)

    def middle(s, c):
        x = mid_ref[:, s].astype(F32).reshape(N, 128)
        n, i = rows_norm(x)
        mid_norm[s] = n
        mid_inv[s] = jnp.broadcast_to(i, n.shape)
        mid_t[s] = n.T.astype(BF16)
        gate[s] = jax.nn.sigmoid(dot(n.astype(BF16), gw_ref[...], 1, 0))
        return c

    lax.fori_loop(0, 16, middle, 0)

    batch(send_a, recv_a, 0).wait_recv()

    def unpack_left(b, c):
        for h in range(4):
            e = recv_a[2 * h * 16 + b].astype(F32)[:8]
            o = recv_a[(2 * h + 1) * 16 + b].astype(F32)[:8]
            lt[rows_at(b * 16, 16, 16), h * 128:(h + 1) * 128] = (
                jnp.concatenate(swap2(e, o), axis=0).astype(BF16))
        return c

    def unpack_right(r, c):
        for g in range(4):
            outs = swap4([recv_a[r * 16 + 4 * g + t].astype(F32)[8:] for t in range(4)])
            rt[rows_at(r * 32, 32, 32), g * 128:(g + 1) * 128] = (
                jnp.concatenate(outs, axis=0).astype(BF16))
        return c

    lax.fori_loop(0, 16, unpack_left, 0)
    lax.fori_loop(0, 8, unpack_right, 0)
    for h in range(4):
        tri[h * 128:(h + 1) * 128, :] = dot(lt[:, h * 128:(h + 1) * 128], rt[...], 0, 0)

    def pack_tri(r, c):
        for g in range(4):
            outs = swap4([
                tri[rows_at(r * 64 + 16 * v, 16, 16), g * 128:(g + 1) * 128] for v in range(4)])
            for t in range(4):
                send_b[r * 16 + 4 * g + t] = outs[t].astype(BF16)
        return c

    lax.fori_loop(0, 8, pack_tri, 0)

    def send_tri(o, c):
        p = lax.rem(me + o, N)
        copy(send_b.at[p], recv_b.at[me], 1, p).start()
        return c

    lax.fori_loop(1, N, send_tri, 0)
    recv_b[me] = send_b[me]

    batch(send_b, recv_b, 1).wait_recv()
    widen(recv_b)

    def heads(s, c):
        at = pl.ds(s, N, stride=16)
        x = wide[at, :]
        centred = x - jnp.mean(x, axis=0, keepdims=True)
        inverse = lax.rsqrt(jnp.mean(centred * centred, axis=0, keepdims=True) + epsilon)
        normed = centred * inverse
        tri_in[s] = normed.astype(BF16)
        tri_t[s] = normed.T.astype(BF16)
        back = (cot_ref[:, s].astype(F32).reshape(N, 128) * gate[s]).astype(BF16)
        head_back[s] = back
        up = dot(ow_ref[...], back, 1, 1)
        first = jnp.mean(up, axis=0, keepdims=True)
        second = jnp.mean(up * normed, axis=0, keepdims=True)
        wide[at, :] = inverse * (up - first - normed * second)
        return c

    lax.fori_loop(0, 16, heads, 0)
    spread(send_c, recv_c, 2)

    sums[...] = jnp.zeros_like(sums)

    def rest(s, c):
        g = gate[s]
        h = dot(tri_t[s], ow_ref[...], 1, 0)
        update_ref[:, s] = (g * h).astype(BF16).reshape(4, 32, 128)
        back = (cot_ref[:, s].astype(F32).reshape(N, 128) * h * g * (1.0 - g)).astype(BF16)
        sums[0:128, :] += dot(mid_t[s], back, 1, 0)
        sums[128:256, :] += dot(tri_in[s], head_back[s], 1, 0)
        up = dot(back, gw_ref[...], 1, 1)
        gmid_ref[:, s] = rows_back(mid_norm[s], mid_inv[s], up).astype(BF16).reshape(4, 32, 128)
        return c

    lax.fori_loop(0, 16, rest, 0)

    def reduce_start(src, recv, k, low, count):
        def step(o, c):
            t = lax.rem(me + o, count)
            @pl.when(low + t != me)
            def _():
                copy(src.at[rows_at(t * 8, 8, 8)], recv.at[me], k, low + t).start()
            return c
        lax.fori_loop(0, count, step, 0)

    def mine(low, count):
        return jnp.logical_and(me >= low, me < low + count)

    def reduce_end(src, recv, total, whole, k, low, count):
        @pl.when(mine(low, count))
        def _():
            batch(recv, recv, k).wait_recv()
            recv[me] = src[rows_at((me - low) * 8, 8, 8), :]
            total[...] = jnp.sum(recv[...], axis=0)
            whole[rows_at((me - low) * 8, 8, 8), :] = total[...]

            def step(o, c):
                p = lax.rem(me + o, N)
                copy(total, whole.at[rows_at((me - low) * 8, 8, 8)], k + 1, p).start()
                return c

            lax.fori_loop(1, N, step, 0)

    def spread_end(recv, whole, k, low, count):
        part = pl.ds(0, (count - 1) * 8)
        @pl.when(mine(low, count))
        def _():
            copy(whole.at[part], whole.at[part], k + 1, lax.rem(me + 1, N)).wait_recv()
        @pl.when(jnp.logical_not(mine(low, count)))
        def _():
            copy(whole, whole, k + 1, lax.rem(me + 1, N)).wait_recv()

    def sends_end(src, recv, k, low, count):
        part = pl.ds(0, (count - 1) * 8)
        @pl.when(mine(low, count))
        def _():
            copy(src.at[part], src.at[part], k, lax.rem(me + 1, N)).wait_send()
            batch(recv, recv, k + 1).wait_send()
        @pl.when(jnp.logical_not(mine(low, count)))
        def _():
            copy(src, src, k, lax.rem(me + 1, N)).wait_send()

    reduce_start(sums, early_recv, 4, 64, 32)

    batch(send_c, recv_c, 2).wait_recv()

    def unpack_tb(r, c):
        for g in range(4):
            outs = swap4([recv_c[r * 16 + 4 * g + t].astype(F32) for t in range(4)])
            for v in range(4):
                tb[rows_at(r * 64 + 16 * v, 16, 16), g * 128:(g + 1) * 128] = outs[v].astype(BF16)
        return c

    lax.fori_loop(0, 8, unpack_tb, 0)
    for h in range(4):
        at = slice(h * 128, (h + 1) * 128)
        lb[:, at] = dot(rt[...], tb[at, :], 1, 1)
        rb[:, at] = dot(lt[...], tb[:, at], 1, 0)

    def pack_left(b, c):
        for h in range(4):
            tile = lb[rows_at(b * 16, 16, 16), h * 128:(h + 1) * 128]
            e, o = swap2(tile[:8], tile[8:])
            wide[rows_at((2 * h * 16 + b) * 16, 8, 8), :] = e
            wide[rows_at(((2 * h + 1) * 16 + b) * 16, 8, 8), :] = o
        return c

    def pack_right(r, c):
        for g in range(4):
            outs = swap4([
                rb[rows_at(r * 32 + 8 * v, 8, 8), g * 128:(g + 1) * 128] for v in range(4)])
            for t in range(4):
                wide[rows_at((r * 16 + 4 * g + t) * 16 + 8, 8, 8), :] = outs[t]
        return c

    lax.fori_loop(0, 16, pack_left, 0)
    lax.fori_loop(0, 8, pack_right, 0)
    spread(send_d, recv_d, 3)

    reduce_end(sums, early_recv, early_total, early_all, 4, 64, 32)

    batch(send_d, recv_d, 3).wait_recv()
    widen(recv_d)
    late_sums[...] = jnp.zeros_like(late_sums)

    def back_step(q, c):
        for side, (normed, inverse, inputs, w_ref) in enumerate(
                ((norm_l, inv_l, in_l, lw_ref), (norm_r, inv_r, in_r, rw_ref))):
            up = wide[pl.ds(side * 8 + q, N, stride=16), :]
            linear, switch = lin[side * 8 + q], sw[side * 8 + q]
            grads = jnp.concatenate(
                [up * switch, up * linear * switch * (1.0 - switch)], axis=0).astype(BF16)
            late_sums[side * 256:(side + 1) * 256, :] += dot(grads, inputs[q], 1, 0)
            input_up = dot(w_ref[...], grads, 1, 0).T
            out = rows_back(chunk(normed, q, side), chunk(inverse, q, side), input_up)
            if side == 0:
                for h in range(2):
                    norm_l[pl.ds(q + 8 * h, 64, stride=16), :] = out[h * 64:(h + 1) * 64]
            else:
                for h in range(4):
                    norm_r[pl.ds(q + 8 * h, 32, stride=32), :] = out[h * 32:(h + 1) * 32]
        return c

    lax.fori_loop(0, 8, back_step, 0)
    reduce_start(late_sums, late_recv, 6, 0, 64)

    def round_step(t, c):
        at = rows_at(t * 128, 128, 128)
        gleft_ref[at, :] = norm_l[at, :].astype(BF16)
        gright_ref[at, :] = norm_r[at, :].astype(BF16)
        return c

    lax.fori_loop(0, 8, round_step, 0)
    reduce_end(late_sums, late_recv, late_total, late_all, 6, 0, 64)
    spread_end(early_recv, early_all, 4, 64, 32)
    dgate_ref[...] = early_all[0:128, :]
    dout_ref[...] = early_all[128:256, :]
    spread_end(late_recv, late_all, 6, 0, 64)
    dleft_ref[...] = late_all[0:256, :].T
    dright_ref[...] = late_all[256:512, :].T

    for k, (send, recv) in enumerate(
            ((send_a, recv_a), (send_b, recv_b), (send_c, recv_c), (send_d, recv_d))):
        batch(send, recv, k).wait_send()
    sends_end(sums, early_recv, 4, 64, 32)
    sends_end(late_sums, late_recv, 6, 0, 64)


def per_device(left, right, middle, cotangent, lw, rw, gw, ow):
    tile = (N, 16, 128)
    scratch = (
        [((2048, 128), F32)] + [(tile, BF16)] * 8
        + [((1024, 128), F32)] * 4 + [((8, 128, 128), BF16)] * 2 + [((16, 128, 128), F32)] * 2
        + [((256, 128), BF16)] * 2 + [((16, 128, 128), F32)] * 2 + [((16, 128, 128), BF16)]
        + [((16, 128, 128), F32)] + [((16, 128, 128), BF16)] * 3
        + [((256, 512), BF16)] * 2 + [((512, 512), F32), ((512, 512), BF16)] + [((256, 512), F32)] * 2
        + [((256, 128), F32), ((512, 128), F32)] + [((N, 8, 128), F32)] * 2
        + [((8, 128), F32)] * 2 + [((256, 128), F32), ((512, 128), F32)]
    )
    vmem = pl.BlockSpec(memory_space=pltpu.VMEM)
    outs = pl.pallas_call(
        kernel,
        out_shape=[
            jax.ShapeDtypeStruct((4, 16, 32, 128), BF16),
            jax.ShapeDtypeStruct((1024, 128), BF16),
            jax.ShapeDtypeStruct((1024, 128), BF16),
            jax.ShapeDtypeStruct((4, 16, 32, 128), BF16),
            jax.ShapeDtypeStruct((128, 256), F32),
            jax.ShapeDtypeStruct((128, 256), F32),
            jax.ShapeDtypeStruct((128, 128), F32),
            jax.ShapeDtypeStruct((128, 128), F32),
        ],
        in_specs=[vmem] * 8,
        out_specs=[vmem] * 8,
        scratch_shapes=[pltpu.VMEM(s, t) for s, t in scratch] + [pltpu.SemaphoreType.DMA((16,))],
        compiler_params=pltpu.CompilerParams(
            collective_id=0, has_side_effects=True, vmem_limit_bytes=48 * 2**20),
    )(
        left.reshape(1024, 128), right.reshape(1024, 128),
        middle.reshape(4, 16, 32, 128), cotangent.reshape(4, 16, 32, 128), lw, rw, gw, ow,
    )
    return (
        outs[0].reshape(64, 32, 128), outs[1].reshape(64, 16, 128),
        outs[2].reshape(32, 32, 128), outs[3].reshape(64, 32, 128), *outs[4:],
    )


def solution(mesh):
    over_i = P(("rep", "rows"), "blk", None)
    over_j = P(("rep", "blk"), "rows", None)
    part = P("rep", None)
    return jax.shard_map(
        per_device,
        mesh=mesh,
        in_specs=(over_i, over_j, over_i, over_i, P(), P(), P(), P()),
        out_specs=(over_i, over_i, over_j, over_i, part, part, part, part),
        check_vma=False,
    )
```

time: 649 us -> 128 us (0.20)
  waiting for transfers between devices: 533 us -> 0 us
  Pallas kernels: 0 us -> 114 us
  local copies, waits for them, and re-layouts: 53.3 us -> 12.7 us
  matrix products: 31.5 us -> 0 us
  other arithmetic: 15.3 us -> 0 us
  between operations: 14.2 us -> 0.66 us
    psum x1 -> x0, waiting for transfers between devices: 219 us -> none  [per_device(): lax.psum((left_part, right_part, gate_part, output_part), ('rows', 'blk'))]
    all_gather x2 -> x0, waiting for transfers between devices: 169 us -> none  [the longest x1 118 us: per_device(): left_whole = lax.all_gather(left_slab, 'blk', axis=1, tiled=True)]
    reduce_scatter x2 -> x0, waiting for transfers between devices: 145 us -> none  [the longest x1 96 us: per_device(): lax.psum_scatter(jnp.einsum('ijc,jkc->kic', tri_back, partner, preferred_...]
    pallas_call x0 -> x1, Pallas kernels: none -> 114 us  [per_device(): pl.pallas_call(kernel, out_shape=[jax.ShapeDtypeStruct((4, 16, 32, 128),...]
    dot_general x15 -> x0, matrix products: 31.5 us -> none  [the longest x4 7.36 us: outer_sum(): jnp.einsum('rc,rd->cd', flat_in, flat_back, preferred_element_type=jnp.fl...]
    all_gather x2 -> x0, local copies, waits for them, and re-layouts: 19 us -> none  [the longest x1 15.6 us: per_device(): left_whole = lax.all_gather(left_slab, 'blk', axis=1, tiled=True)]
    dot_general x3 -> x0, local copies, waits for them, and re-layouts: 14.4 us -> none  [the longest x1 6.9 us: per_device(): jnp.einsum('ijc,jkc->kic', tri_back, partner, preferred_element_type=jnp....]
    convert_element_type x6 -> x0, other arithmetic: 7.85 us -> none  [the longest x1 1.95 us: per_device(): normalize_back(middle_norm, middle_inverse, middle_up).astype(jnp.bfloat16)]
  transfers between devices with their start and end apart: 5 -> 0, of which waited for: 5 -> 0; matrix products, arithmetic and copies ran while one was open for 7% -> 0% of each run, Pallas kernels for 0% -> 0%
where the time goes in v2:
time: 128 us; the launch traced here: 127 us
  Pallas kernels  114 us (89%)
  local copies, waits for them, and re-layouts  12.7 us (10%)
    pallas_call x1, Pallas kernels, per_device(): pl.pallas_call(kernel, out_shape=[jax.ShapeDtypeStruct((4, 16, 32, 128),...  114 us
    unnamed x24, local copies, waits for them, and re-layouts  12.7 us

profile of v2, /device:TPU:2, one launch (start us, length us, event | category | flops | bytes accessed | tf_op | source)
XLA Modules:
  0.0 127.3 jit_solution(15314653015960231610)
XLA Ops:
  0.6 0.0 copy-start
  0.6 1.0 copy-done
  1.7 0.0 copy-start.1
  1.7 1.0 copy-done.1
  2.7 0.0 copy-start.2
  2.7 0.9 copy-done.2
  3.7 0.0 copy-start.3
  3.7 0.9 copy-done.3
  4.6 0.0 copy-start.4
  4.6 0.8 copy-done.4
  5.5 0.0 copy-start.5
  5.5 0.8 copy-done.5
  6.3 0.0 copy-start.6
  6.3 0.8 copy-done.6
  7.1 0.0 copy-start.7
  7.1 0.8 copy-done.7
  7.8 113.9 %shard_map.143 = (bf16[4,16,32,128]{3,2,1,0:T(8,128)(2,1)S(1)}, bf16[1024,128]{1,0:T(8,128)(2,1)S(1)}, bf16[1024,128]{1,0:T(8,128)(2,1)S(1)}, bf16[4,16,32,128]{...) custom-call(bf16[1024,128]{1,0:T(8,128)(2,1)S(1)} %bitcast.12, ...), custom_call_target="tpu_custom_call" | custom-call | tf_op jit(solution)/shard_map/pallas_call | solution.py:368
  121.7 0.8 copy.24
  122.5 0.7 copy.25
  123.2 0.7 copy.26
  123.9 0.8 copy.27
  124.7 0.7 copy.28
  125.4 0.7 copy.29
  126.0 0.6 copy.30
  126.6 0.6 copy.31
Async XLA Ops:
  0.6 1.0 copy-start
  1.7 1.0 copy-start.1
  2.7 0.9 copy-start.2
  3.7 0.9 copy-start.3
  4.6 0.8 copy-start.4
  5.5 0.8 copy-start.5
  6.3 0.8 copy-start.6
  7.1 0.8 copy-start.7

commit v3 on v2

--- a/solution.py
+++ b/solution.py
@@ -56,17 +56,31 @@
 
 
 def kernel(
+    left_hbm, right_hbm, mid_hbm, cot_hbm, lw_hbm, rw_hbm, gw_hbm, ow_hbm,
+    update_hbm, gleft_hbm, gright_hbm, gmid_hbm, dleft_hbm, dright_hbm, dgate_hbm, dout_hbm,
+    update_ref, gleft_ref, gright_ref, gmid_ref, dleft_ref, dright_ref, dgate_ref, dout_ref,
     left_ref, right_ref, mid_ref, cot_ref, lw_ref, rw_ref, gw_ref, ow_ref,
-    update_ref, gleft_ref, gright_ref, gmid_ref, dleft_ref, dright_ref, dgate_ref, dout_ref,
     wide, send_a, send_b, send_c, send_d, recv_a, recv_b, recv_c, recv_d,
     norm_l, norm_r, inv_l, inv_r, in_l, in_r, lin, sw,
     lwt, rwt, mid_norm, mid_inv, mid_t, gate, head_back, tri_in, tri_t,
     lt, rt, tri, tb, lb, rb,
-    sums, late_sums, early_recv, late_recv, early_total, late_total, early_all, late_all,
-    sems,
+    grads_l, grads_r, sums, late_sums, early_send, late_send, early_recv, late_recv,
+    early_total, late_total, early_all, late_all, sems, fetch_sems, store_sems,
 ):
     me = lax.axis_index("rows") * 16 + lax.axis_index("blk")
     barrier = pltpu.get_barrier_semaphore()
+    fetches = [
+        pltpu.make_async_copy(src, dst, fetch_sems.at[n]) for n, (src, dst) in enumerate((
+            (left_hbm, left_ref), (right_hbm, right_ref), (lw_hbm, lw_ref), (rw_hbm, rw_ref),
+            (mid_hbm, mid_ref), (gw_hbm, gw_ref), (cot_hbm, cot_ref), (ow_hbm, ow_ref)))]
+    for fetch in fetches:
+        fetch.start()
+    stores = []
+
+    def store(*pairs):
+        for src, dst in pairs:
+            stores.append(pltpu.make_async_copy(src, dst, store_sems.at[len(stores)]))
+            stores[-1].start()
 
     def copy(src, dst, k, p):
         return pltpu.make_async_remote_copy(
@@ -99,6 +113,8 @@
             return c
         lax.fori_loop(0, 8, step, 0)
 
+    for fetch in fetches[:4]:
+        fetch.wait()
     lwt[...] = lw_ref[...].astype(F32).T.astype(BF16)
     rwt[...] = rw_ref[...].astype(F32).T.astype(BF16)
 
@@ -142,6 +158,8 @@
         gate[s] = jax.nn.sigmoid(dot(n.astype(BF16), gw_ref[...], 1, 0))
         return c
 
+    for fetch in fetches[4:]:
+        fetch.wait()
     lax.fori_loop(0, 16, middle, 0)
 
     batch(send_a, recv_a, 0).wait_recv()
@@ -220,54 +238,59 @@
         return c
 
     lax.fori_loop(0, 16, rest, 0)
-
-    def reduce_start(src, recv, k, low, count):
-        def step(o, c):
-            t = lax.rem(me + o, count)
-            @pl.when(low + t != me)
+    store((update_ref, update_hbm), (gmid_ref, gmid_hbm))
+
+    def owned(step, base):
+        place = lax.rem(me, step) - base
+        return jnp.logical_and(place >= 0, place < 2), (me // step) * 2 + place
+
+    def reduce_start(src, send, recv, k, step, base, count):
+        send[...] = src[...].astype(BF16)
+
+        def one(o, c):
+            t = lax.rem(me // (N // count) + o, count)
+            p = (t // 2) * step + base + lax.rem(t, 2)
+            @pl.when(p != me)
             def _():
-                copy(src.at[rows_at(t * 8, 8, 8)], recv.at[me], k, low + t).start()
+                copy(send.at[rows_at(t * 16, 16, 16)], recv.at[me], k, p).start()
             return c
-        lax.fori_loop(0, count, step, 0)
-
-    def mine(low, count):
-        return jnp.logical_and(me >= low, me < low + count)
-
-    def reduce_end(src, recv, total, whole, k, low, count):
-        @pl.when(mine(low, count))
+
+        lax.fori_loop(0, count, one, 0)
+
+    def reduce_end(send, recv, total, whole, k, step, base):
+        owner, t = owned(step, base)
+        @pl.when(owner)
         def _():
+            at = rows_at(t * 16, 16, 16)
             batch(recv, recv, k).wait_recv()
-            recv[me] = src[rows_at((me - low) * 8, 8, 8), :]
-            total[...] = jnp.sum(recv[...], axis=0)
-            whole[rows_at((me - low) * 8, 8, 8), :] = total[...]
-
-            def step(o, c):
-                p = lax.rem(me + o, N)
-                copy(total, whole.at[rows_at((me - low) * 8, 8, 8)], k + 1, p).start()
+            recv[me] = send[at, :]
+            total[...] = jnp.sum(recv[...].astype(F32), axis=0).astype(BF16)
+            whole[at, :] = total[...]
+
+            def one(o, c):
+                copy(total, whole.at[at], k + 1, lax.rem(me + o, N)).start()
                 return c
 
-            lax.fori_loop(1, N, step, 0)
-
-    def spread_end(recv, whole, k, low, count):
-        part = pl.ds(0, (count - 1) * 8)
-        @pl.when(mine(low, count))
+            lax.fori_loop(1, N, one, 0)
+
+    def by_owner(ref, k, step, base, count, wait):
+        owner, _ = owned(step, base)
+        for own, rows in ((owner, count * 16 - 16), (jnp.logical_not(owner), count * 16)):
+            @pl.when(own)
+            def _():
+                wait(copy(ref.at[pl.ds(0, rows)], ref.at[pl.ds(0, rows)], k, lax.rem(me + 1, N)))
+
+    def spread_end(whole, k, step, base, count):
+        by_owner(whole, k + 1, step, base, count, lambda c: c.wait_recv())
+
+    def sends_end(send, recv, k, step, base, count):
+        by_owner(send, k, step, base, count, lambda c: c.wait_send())
+        @pl.when(owned(step, base)[0])
         def _():
-            copy(whole.at[part], whole.at[part], k + 1, lax.rem(me + 1, N)).wait_recv()
-        @pl.when(jnp.logical_not(mine(low, count)))
-        def _():
-            copy(whole, whole, k + 1, lax.rem(me + 1, N)).wait_recv()
-
-    def sends_end(src, recv, k, low, count):
-        part = pl.ds(0, (count - 1) * 8)
-        @pl.when(mine(low, count))
-        def _():
-            copy(src.at[part], src.at[part], k, lax.rem(me + 1, N)).wait_send()
             batch(recv, recv, k + 1).wait_send()
-        @pl.when(jnp.logical_not(mine(low, count)))
-        def _():
-            copy(src, src, k, lax.rem(me + 1, N)).wait_send()
-
-    reduce_start(sums, early_recv, 4, 64, 32)
+
+    early, late = (16, 4), (8, 0)
+    reduce_start(sums, early_send, early_recv, 4, *early, 16)
 
     batch(send_c, recv_c, 2).wait_recv()
 
@@ -304,21 +327,30 @@
     lax.fori_loop(0, 8, pack_right, 0)
     spread(send_d, recv_d, 3)
 
-    reduce_end(sums, early_recv, early_total, early_all, 4, 64, 32)
+    reduce_end(early_send, early_recv, early_total, early_all, 4, *early)
 
     batch(send_d, recv_d, 3).wait_recv()
     widen(recv_d)
     late_sums[...] = jnp.zeros_like(late_sums)
 
-    def back_step(q, c):
-        for side, (normed, inverse, inputs, w_ref) in enumerate(
-                ((norm_l, inv_l, in_l, lw_ref), (norm_r, inv_r, in_r, rw_ref))):
+    sides = ((norm_l, inv_l, in_l, lw_ref, grads_l), (norm_r, inv_r, in_r, rw_ref, grads_r))
+
+    def pre_grads(q, c):
+        for side, (_, _, inputs, _, grads) in enumerate(sides):
             up = wide[pl.ds(side * 8 + q, N, stride=16), :]
             linear, switch = lin[side * 8 + q], sw[side * 8 + q]
-            grads = jnp.concatenate(
+            joined = jnp.concatenate(
                 [up * switch, up * linear * switch * (1.0 - switch)], axis=0).astype(BF16)
-            late_sums[side * 256:(side + 1) * 256, :] += dot(grads, inputs[q], 1, 0)
-            input_up = dot(w_ref[...], grads, 1, 0).T
+            grads[q] = joined
+            late_sums[side * 256:(side + 1) * 256, :] += dot(joined, inputs[q], 1, 0)
+        return c
+
+    lax.fori_loop(0, 8, pre_grads, 0)
+    reduce_start(late_sums, late_send, late_recv, 6, *late, 32)
+
+    def back_step(q, c):
+        for side, (normed, inverse, _, w_ref, grads) in enumerate(sides):
+            input_up = dot(w_ref[...], grads[q], 1, 0).T
             out = rows_back(chunk(normed, q, side), chunk(inverse, q, side), input_up)
             if side == 0:
                 for h in range(2):
@@ -329,7 +361,6 @@
         return c
 
     lax.fori_loop(0, 8, back_step, 0)
-    reduce_start(late_sums, late_recv, 6, 0, 64)
 
     def round_step(t, c):
         at = rows_at(t * 128, 128, 128)
@@ -338,54 +369,75 @@
         return c
 
     lax.fori_loop(0, 8, round_step, 0)
-    reduce_end(late_sums, late_recv, late_total, late_all, 6, 0, 64)
-    spread_end(early_recv, early_all, 4, 64, 32)
-    dgate_ref[...] = early_all[0:128, :]
-    dout_ref[...] = early_all[128:256, :]
-    spread_end(late_recv, late_all, 6, 0, 64)
-    dleft_ref[...] = late_all[0:256, :].T
-    dright_ref[...] = late_all[256:512, :].T
+    store((gleft_ref, gleft_hbm), (gright_ref, gright_hbm))
+    reduce_end(late_send, late_recv, late_total, late_all, 6, *late)
+    spread_end(early_all, 4, *early, 16)
+    dgate_ref[...] = early_all[0:128, :].astype(F32)
+    dout_ref[...] = early_all[128:256, :].astype(F32)
+    spread_end(late_all, 6, *late, 32)
+    dleft_ref[...] = late_all[0:256, :].astype(F32).T
+    dright_ref[...] = late_all[256:512, :].astype(F32).T
+    store((dgate_ref, dgate_hbm), (dout_ref, dout_hbm), (dleft_ref, dleft_hbm), (dright_ref, dright_hbm))
 
     for k, (send, recv) in enumerate(
             ((send_a, recv_a), (send_b, recv_b), (send_c, recv_c), (send_d, recv_d))):
         batch(send, recv, k).wait_send()
-    sends_end(sums, early_recv, 4, 64, 32)
-    sends_end(late_sums, late_recv, 6, 0, 64)
+    sends_end(early_send, early_recv, 4, *early, 16)
+    sends_end(late_send, late_recv, 6, *late, 32)
+    for one in stores:
+        one.wait()
+
+
+def store_kernel(*refs):
+    sources, targets, held, sems = refs[:8], refs[8:16], refs[16:24], refs[24]
+    reads = [pltpu.make_async_copy(s, h, sems.at[n]) for n, (s, h) in enumerate(zip(sources, held))]
+    writes = [pltpu.make_async_copy(h, t, sems.at[8 + n]) for n, (h, t) in enumerate(zip(held, targets))]
+    for read in reads:
+        read.start()
+    for read, write in zip(reads, writes):
+        read.wait()
+        write.start()
+    for write in writes:
+        write.wait()
 
 
 def per_device(left, right, middle, cotangent, lw, rw, gw, ow):
     tile = (N, 16, 128)
+    pairs, flat, mids = (1024, 128), ((1024, 128), BF16), ((4, 16, 32, 128), BF16)
+    results = [mids, flat, flat, mids] + [((128, 256), F32)] * 2 + [((128, 128), F32)] * 2
+    shapes = [jax.ShapeDtypeStruct(s, t) for s, t in results]
     scratch = (
-        [((2048, 128), F32)] + [(tile, BF16)] * 8
-        + [((1024, 128), F32)] * 4 + [((8, 128, 128), BF16)] * 2 + [((16, 128, 128), F32)] * 2
+        results + [flat, flat, mids, mids] + [((128, 256), BF16)] * 2 + [((128, 128), BF16)] * 2
+        + [((2048, 128), F32)] + [(tile, BF16)] * 8
+        + [(pairs, F32)] * 4 + [((8, 128, 128), BF16)] * 2 + [((16, 128, 128), F32)] * 2
         + [((256, 128), BF16)] * 2 + [((16, 128, 128), F32)] * 2 + [((16, 128, 128), BF16)]
         + [((16, 128, 128), F32)] + [((16, 128, 128), BF16)] * 3
         + [((256, 512), BF16)] * 2 + [((512, 512), F32), ((512, 512), BF16)] + [((256, 512), F32)] * 2
-        + [((256, 128), F32), ((512, 128), F32)] + [((N, 8, 128), F32)] * 2
-        + [((8, 128), F32)] * 2 + [((256, 128), F32), ((512, 128), F32)]
+        + [((8, 256, 128), BF16)] * 2
+        + [((256, 128), F32), ((512, 128), F32), ((256, 128), BF16), ((512, 128), BF16)]
+        + [(tile, BF16)] * 2 + [((16, 128), BF16)] * 2 + [((256, 128), BF16), ((512, 128), BF16)]
     )
-    vmem = pl.BlockSpec(memory_space=pltpu.VMEM)
     outs = pl.pallas_call(
         kernel,
-        out_shape=[
-            jax.ShapeDtypeStruct((4, 16, 32, 128), BF16),
-            jax.ShapeDtypeStruct((1024, 128), BF16),
-            jax.ShapeDtypeStruct((1024, 128), BF16),
-            jax.ShapeDtypeStruct((4, 16, 32, 128), BF16),
-            jax.ShapeDtypeStruct((128, 256), F32),
-            jax.ShapeDtypeStruct((128, 256), F32),
-            jax.ShapeDtypeStruct((128, 128), F32),
-            jax.ShapeDtypeStruct((128, 128), F32),
-        ],
-        in_specs=[vmem] * 8,
-        out_specs=[vmem] * 8,
-        scratch_shapes=[pltpu.VMEM(s, t) for s, t in scratch] + [pltpu.SemaphoreType.DMA((16,))],
+        out_shape=shapes,
+        in_specs=[pl.BlockSpec(memory_space=pltpu.HBM)] * 8,
+        out_specs=[pl.BlockSpec(memory_space=pltpu.HBM)] * 8,
+        scratch_shapes=[pltpu.VMEM(s, t) for s, t in scratch] + [
+            pltpu.SemaphoreType.DMA((16,)), pltpu.SemaphoreType.DMA((8,)), pltpu.SemaphoreType.DMA((8,))],
         compiler_params=pltpu.CompilerParams(
-            collective_id=0, has_side_effects=True, vmem_limit_bytes=48 * 2**20),
+            collective_id=0, has_side_effects=True, vmem_limit_bytes=61 * 2**20),
     )(
-        left.reshape(1024, 128), right.reshape(1024, 128),
-        middle.reshape(4, 16, 32, 128), cotangent.reshape(4, 16, 32, 128), lw, rw, gw, ow,
+        left.reshape(pairs), right.reshape(pairs),
+        middle.reshape(mids[0]), cotangent.reshape(mids[0]), lw, rw, gw, ow,
     )
+    outs = pl.pallas_call(
+        store_kernel,
+        out_shape=shapes,
+        in_specs=[pl.BlockSpec(memory_space=pltpu.HBM)] * 8,
+        out_specs=[pl.BlockSpec(memory_space=pltpu.HBM)] * 8,
+        scratch_shapes=[pltpu.VMEM(s, t) for s, t in results] + [pltpu.SemaphoreType.DMA((16,))],
+        compiler_params=pltpu.CompilerParams(vmem_limit_bytes=61 * 2**20),
+    )(*outs)
     return (
         outs[0].reshape(64, 32, 128), outs[1].reshape(64, 16, 128),
         outs[2].reshape(32, 32, 128), outs[3].reshape(64, 32, 128), *outs[4:],

time: 128 us -> 109 us (0.85)
  local copies, waits for them, and re-layouts: 12.7 us -> 0 us
  Pallas kernels: 114 us -> 108 us
    unnamed x24 -> x0, local copies, waits for them, and re-layouts: 12.7 us -> none
    pallas_call x1 -> x2, Pallas kernels: 114 us -> 108 us  [the longest x1 106 us: per_device(): pl.pallas_call(kernel, out_shape=shapes, in_specs=[pl.BlockSpec(memory_sp...]
where the time goes in v3:
time: 109 us
  Pallas kernels  108 us (99%)
    pallas_call x1, Pallas kernels, per_device(): pl.pallas_call(kernel, out_shape=shapes, in_specs=[pl.BlockSpec(memory_sp...  106 us
    pallas_call x1, Pallas kernels, per_device(): pl.pallas_call(store_kernel, out_shape=shapes, in_specs=[pl.BlockSpec(mem...  2.44 us

profile of v3, /device:TPU:2, one launch (start us, length us, event | category | flops | bytes accessed | tf_op | source)
XLA Modules:
  0.0 109.0 jit_solution(8074843484826354623)
XLA Ops:
  0.6 105.9 %shard_map.143 = (bf16[4,16,32,128]{3,2,1,0:T(8,128)(2,1)}, bf16[1024,128]{1,0:T(8,128)(2,1)}, bf16[1024,128]{1,0:T(8,128)(2,1)}, bf16[4,16,32,128]{3,2,1,0:T(8,...) custom-call(bf16[1024,128]{1,0:T(8,128)(2,1)} %bitcast.10, ...), custom_call_target="tpu_custom_call" | custom-call | tf_op jit(solution)/shard_map/pallas_call | solution.py:420
  106.6 2.4 %shard_map.144 = (bf16[4,16,32,128]{3,2,1,0:T(8,128)(2,1)}, bf16[1024,128]{1,0:T(8,128)(2,1)}, bf16[1024,128]{1,0:T(8,128)(2,1)}, bf16[4,16,32,128]{3,2,1,0:T(8,...) custom-call(bf16[4,16,32,128]{3,2,1,0:T(8,128)(2,1)} %get-tuple-element.24.refs_0_, ...), custom_call_target="tpu_custom_call" | custom-call | tf_op jit(solution)/shard_map/pallas_call | solution.py:433

commit v4 on v3

v4 whole, which is shorter than its diff:
```python
import jax
import jax.numpy as jnp
from jax import lax
from jax.experimental import pallas as pl
from jax.experimental.pallas import tpu as pltpu
from jax.sharding import PartitionSpec as P

epsilon = 1e-05
F32 = jnp.float32
BF16 = jnp.bfloat16
MESH = pl.DeviceIdType.MESH
N = 128


def partner(p):
    return {"rows": p // 16, "blk": lax.rem(p, 16)}


def rows_norm(x):
    centred = x - jnp.mean(x, axis=-1, keepdims=True)
    inverse = lax.rsqrt(jnp.mean(centred * centred, axis=-1, keepdims=True) + epsilon)
    return centred * inverse, inverse


def rows_back(normed, inverse, up):
    first = jnp.mean(up, axis=-1, keepdims=True)
    second = jnp.mean(up * normed, axis=-1, keepdims=True)
    return inverse * (up - first - normed * second)


def dot(a, b, ca, cb):
    return lax.dot_general(a, b, (((ca,), (cb,)), ((), ())), preferred_element_type=F32)


def swap2(a, b):
    low = lax.broadcasted_iota(jnp.int32, a.shape, 1) < 64
    return (
        jnp.where(low, a, pltpu.roll(b, 64, 1)),
        jnp.where(low, pltpu.roll(a, 64, 1), b),
    )


def swap4(xs):
    y0, y2 = swap2(xs[0], xs[2])
    y1, y3 = swap2(xs[1], xs[3])
    low = (lax.broadcasted_iota(jnp.int32, y0.shape, 1) & 32) == 0
    outs = []
    for a, b in ((y0, y1), (y2, y3)):
        outs.append(jnp.where(low, a, pltpu.roll(b, 32, 1)))
        outs.append(jnp.where(low, pltpu.roll(a, 96, 1), b))
    return outs


def rows_at(start, size, step):
    return pl.ds(pl.multiple_of(start, step), size)


def kernel(
    left_hbm, right_hbm, mid_hbm, cot_hbm, lw_hbm, rw_hbm, gw_hbm, ow_hbm,
    update_hbm, gleft_hbm, gright_hbm, gmid_hbm, dleft_hbm, dright_hbm, dgate_hbm, dout_hbm,
    update_ref, gleft_ref, gright_ref, gmid_ref, dleft_ref, dright_ref, dgate_ref, dout_ref,
    left_ref, right_ref, mid_ref, cot_ref, lw_ref, rw_ref, gw_ref, ow_ref,
    wide, send_a, send_b, send_c, send_d, recv_a, recv_b, recv_c, recv_d,
    norm_l, norm_r, inv_l, inv_r, in_l, in_r, lin, sw,
    lwt, rwt, mid_norm, mid_inv, mid_t, gate, head_back, tri_in,
    lt, rt, tri, tb, lb, rb,
    grads_l, grads_r, sums, late_sums, early_send, late_send, early_held, late_held,
    early_part, late_part, early_parts, late_parts, early_all, late_all, sems, arrive_sems, fetch_sems, store_sems,
):
    my_row, my_blk = lax.axis_index("rows"), lax.axis_index("blk")
    me = my_row * 16 + my_blk
    barrier = pltpu.get_barrier_semaphore()
    fetches = [
        pltpu.make_async_copy(src, dst, fetch_sems.at[n]) for n, (src, dst) in enumerate((
            (left_hbm, left_ref), (right_hbm, right_ref), (lw_hbm, lw_ref), (rw_hbm, rw_ref),
            (mid_hbm, mid_ref), (gw_hbm, gw_ref), (cot_hbm, cot_ref), (ow_hbm, ow_ref)))]
    for fetch in fetches:
        fetch.start()
    stores = []

    def store(*pairs):
        for src, dst in pairs:
            stores.append(pltpu.make_async_copy(src, dst, store_sems.at[len(stores)]))
            stores[-1].start()

    def copy(src, dst, k, p, arrive=None):
        return pltpu.make_async_remote_copy(
            src_ref=src, dst_ref=dst, send_sem=sems.at[2 * k],
            recv_sem=sems.at[2 * k + 1] if arrive is None else arrive,
            device_id=partner(p), device_id_type=MESH)

    def greet(o, c):
        pl.semaphore_signal(
            barrier, inc=1, device_id=partner(lax.rem(me + o, N)), device_id_type=MESH)
        return c

    lax.fori_loop(1, N, greet, 0)

    def pair(g):
        return lax.rem(me // 32 + g, 4), lax.rem(me // 32 + 4 - g, 4)

    def spread(send, recv, k, fill=True):
        if fill:
            recv[me] = wide[rows_at(me * 16, 16, 16), :].astype(BF16)
        else:
            recv[me] = send[me]
        for g in range(4):
            def step(o, c):
                p = pair(g)[0] * 32 + lax.rem(me + o, 32)
                if fill:
                    send[p] = wide[rows_at(p * 16, 16, 16), :].astype(BF16)
                copy(send.at[p], recv.at[me], k, p, arrive_sems.at[4 * k + g]).start()
                return c
            lax.fori_loop(0 if g else 1, 32, step, 0)

    def arrived(recv, k, g):
        part = pl.ds(0, 32 if g else 31)
        copy(recv.at[part], recv.at[part], k, lax.rem(me + 1, N), arrive_sems.at[4 * k + g]).wait_recv()
        return pair(g)[1]

    def widen(recv, k):
        for g in range(4):
            first = arrived(recv, k, g) * 32
            def step(t, c):
                at = first + t * 16
                wide[rows_at(at * 16, 256, 256), :] = (
                    recv[rows_at(at, 16, 16)].astype(F32).reshape(256, 128))
                return c
            lax.fori_loop(0, 2, step, 0)

    for fetch in fetches[:4]:
        fetch.wait()
    lwt[...] = lw_ref[...].astype(F32).T.astype(BF16)
    rwt[...] = rw_ref[...].astype(F32).T.astype(BF16)

    def norm_step(t, c):
        at = rows_at(t * 128, 128, 128)
        for ref, normed, inverse in ((left_ref, norm_l, inv_l), (right_ref, norm_r, inv_r)):
            n, i = rows_norm(ref[at, :].astype(F32))
            normed[at, :] = n
            inverse[at, :] = jnp.broadcast_to(i, n.shape)
        return c

    lax.fori_loop(0, 8, norm_step, 0)

    def chunk(ref, q, side):
        if side == 0:
            return jnp.concatenate([ref[pl.ds(q + 8 * h, 64, stride=16), :] for h in range(2)], axis=0)
        return jnp.concatenate([ref[pl.ds(q + 8 * h, 32, stride=32), :] for h in range(4)], axis=0)

    def project(q, c):
        for side, (normed, inputs, wt) in enumerate(((norm_l, in_l, lwt), (norm_r, in_r, rwt))):
            x = chunk(normed, q, side).astype(BF16)
            inputs[q] = x
            pre = dot(wt[...], x, 1, 1)
            linear, switch = pre[:N], jax.nn.sigmoid(pre[N:])
            lin[side * 8 + q] = linear
            sw[side * 8 + q] = switch
            wide[pl.ds(side * 8 + q, N, stride=16), :] = linear * switch
        return c

    lax.fori_loop(0, 8, project, 0)

    pl.semaphore_wait(barrier, N - 1)
    spread(send_a, recv_a, 0)

    for g in range(4):
        h = arrived(recv_a, 0, g)
        at = rows_at(h * 128, 128, 128)

        def unpack_left(n, c):
            tiles = [[recv_a[h * 32 + 16 * v + n * 4 + u].astype(F32)[:8] for v in range(2)] for u in range(4)]
            outs = [out for e, o in tiles for out in swap2(e, o)]
            lt[rows_at(n * 64, 64, 64), at] = jnp.concatenate(outs, axis=0).astype(BF16)
            return c

        def unpack_right(n, c):
            r = h * 2 + n
            tiles = [recv_a[r * 16 + t].astype(F32)[8:] for t in range(16)]
            outs = [jnp.concatenate(swap4(tiles[4 * v:4 * v + 4]), axis=0) for v in range(4)]
            rt[rows_at(r * 32, 32, 32), :] = jnp.concatenate(outs, axis=1).astype(BF16)
            return c

        lax.fori_loop(0, 4, unpack_left, 0)
        lax.fori_loop(0, 2, unpack_right, 0)

    for h in range(4):
        tri[h * 128:(h + 1) * 128, :] = dot(lt[:, h * 128:(h + 1) * 128], rt[...], 0, 0)

    def pack_tri(r, c):
        rows = tri[rows_at(r * 64, 64, 64), :]
        outs = [swap4([rows[16 * v:16 * v + 16, g * 128:(g + 1) * 128] for v in range(4)]) for g in range(4)]
        for g in range(4):
            for t in range(4):
                send_b[r * 16 + 4 * g + t] = outs[g][t].astype(BF16)
        return c

    lax.fori_loop(0, 8, pack_tri, 0)

    spread(send_b, recv_b, 1, fill=False)

    def middle(q, c):
        slots = (2 * q, 2 * q + 1)
        xs = [mid_ref[:, s].astype(F32).reshape(N, 128) for s in slots]
        norms = [rows_norm(x) for x in xs]
        gates = [jax.nn.sigmoid(dot(n.astype(BF16), gw_ref[...], 1, 0)) for n, _ in norms]
        turned = [n.T.astype(BF16) for n, _ in norms]
        for s, (n, i), g, t in zip(slots, norms, gates, turned):
            mid_norm[s] = n
            mid_inv[s] = jnp.broadcast_to(i, n.shape)
            mid_t[s] = t
            gate[s] = g
        return c

    for fetch in fetches[4:]:
        fetch.wait()
    lax.fori_loop(0, 8, middle, 0)

    widen(recv_b, 1)

    def heads(q, c):
        slots = (2 * q, 2 * q + 1)
        at = [pl.ds(s, N, stride=16) for s in slots]
        xs = [wide[a, :] for a in at]
        backs = [(cot_ref[:, s].astype(F32).reshape(N, 128) * gate[s]).astype(BF16) for s in slots]
        ups = [dot(ow_ref[...], back, 1, 1) for back in backs]
        outs = []
        for x, up in zip(xs, ups):
            centred = x - jnp.mean(x, axis=0, keepdims=True)
            inverse = lax.rsqrt(jnp.mean(centred * centred, axis=0, keepdims=True) + epsilon)
            normed = centred * inverse
            first = jnp.mean(up, axis=0, keepdims=True)
            second = jnp.mean(up * normed, axis=0, keepdims=True)
            outs.append((normed, inverse * (up - first - normed * second)))
        for s, a, back, (normed, out) in zip(slots, at, backs, outs):
            head_back[s] = back
            tri_in[s] = normed.astype(BF16)
            wide[a, :] = out
        return c

    lax.fori_loop(0, 8, heads, 0)
    spread(send_c, recv_c, 2)

    def over_blk(o):
        return my_row * 16 + lax.rem(my_blk + o, 16)

    def sum_scatter(src, send, held, k):
        send[...] = src[...].astype(BF16)
        rows = held.shape[1]
        for o in range(1, 16):
            p = over_blk(o)
            at = rows_at(lax.rem(p, 16) * rows, rows, rows)
            copy(send.at[at], held.at[my_blk], k, p).start()
        held[my_blk] = send[rows_at(my_blk * rows, rows, rows), :]

    def sum_exchange(held, part, parts, k):
        copy(held.at[pl.ds(0, 15)], held.at[pl.ds(0, 15)], k, over_blk(1)).wait_recv()
        part[...] = jnp.sum(held[...].astype(F32), axis=0)
        for o in range(1, 8):
            copy(part, parts.at[my_row], k + 1, lax.rem(me + 16 * o, N)).start()
        parts[my_row] = part[...]

    def sum_spread(parts, whole, k):
        copy(parts.at[pl.ds(0, 7)], parts.at[pl.ds(0, 7)], k + 1, lax.rem(me + 16, N)).wait_recv()
        rows = parts.shape[1]
        at = rows_at(my_blk * rows, rows, rows)
        whole[at, :] = jnp.sum(parts[...], axis=0).astype(BF16)
        for o in range(1, 16):
            copy(whole.at[at], whole.at[at], k + 2, over_blk(o)).start()

    def sum_wait(whole, k):
        most = pl.ds(0, whole.shape[0] // 16 * 15)
        copy(whole.at[most], whole.at[most], k + 2, over_blk(1)).wait_recv()

    def sum_sent(whole, parts, k):
        most = pl.ds(0, whole.shape[0] // 16 * 15)
        copy(whole.at[most], whole.at[most], k, over_blk(1)).wait_send()
        copy(parts.at[pl.ds(0, 7)], parts.at[pl.ds(0, 7)], k + 1, over_blk(1)).wait_send()
        copy(whole.at[most], whole.at[most], k + 2, over_blk(1)).wait_send()

    for g in range(4):
        h = arrived(recv_c, 2, g)
        at = rows_at(h * 128, 128, 128)

        def unpack_tb(n, c):
            r = h * 2 + n
            tiles = [recv_c[r * 16 + t].astype(F32) for t in range(16)]
            outs = [jnp.concatenate(swap4(tiles[4 * v:4 * v + 4]), axis=0) for v in range(4)]
            tb[rows_at(r * 64, 64, 64), :] = jnp.concatenate(outs, axis=1).astype(BF16)
            return c

        lax.fori_loop(0, 2, unpack_tb, 0)
        lb[...] = dot(rt[...], tb[at, :], 1, 1)
        if g == 0:
            rb[...] = dot(lt[:, at], tb[at, :], 1, 0)
        else:
            rb[...] += dot(lt[:, at], tb[at, :], 1, 0)

        def pack_left(n, c):
            tiles = [lb[rows_at((n * 4 + u) * 16, 16, 16), :] for u in range(4)]
            outs = [swap2(tile[:8], tile[8:]) for tile in tiles]
            for u in range(4):
                for v in range(2):
                    wide[rows_at((h * 32 + 16 * v + n * 4 + u) * 16, 8, 8), :] = outs[u][v]
            return c

        lax.fori_loop(0, 4, pack_left, 0)

    def pack_right(r, c):
        rows = rb[rows_at(r * 32, 32, 32), :]
        outs = [swap4([rows[8 * v:8 * v + 8, g * 128:(g + 1) * 128] for v in range(4)]) for g in range(4)]
        for g in range(4):
            for t in range(4):
                wide[rows_at((r * 16 + 4 * g + t) * 16 + 8, 8, 8), :] = outs[g][t]
        return c

    lax.fori_loop(0, 8, pack_right, 0)
    spread(send_d, recv_d, 3)

    sums[...] = jnp.zeros_like(sums)

    def rest(q, c):
        slots = (2 * q, 2 * q + 1)
        gates = [gate[s] for s in slots]
        hs = [dot(tri_in[s].astype(F32).T.astype(BF16), ow_ref[...], 1, 0) for s in slots]
        backs = [
            (cot_ref[:, s].astype(F32).reshape(N, 128) * h * g * (1.0 - g)).astype(BF16)
            for s, h, g in zip(slots, hs, gates)]
        outs = [
            rows_back(mid_norm[s], mid_inv[s], dot(b, gw_ref[...], 1, 1)).astype(BF16)
            for s, b in zip(slots, backs)]
        gate_sum = [dot(mid_t[s], b, 1, 0) for s, b in zip(slots, backs)]
        out_sum = [dot(tri_in[s], head_back[s], 1, 0) for s in slots]
        sums[0:128, :] += gate_sum[0] + gate_sum[1]
        sums[128:256, :] += out_sum[0] + out_sum[1]
        for s, g, h, out in zip(slots, gates, hs, outs):
            update_ref[:, s] = (g * h).astype(BF16).reshape(4, 32, 128)
            gmid_ref[:, s] = out.reshape(4, 32, 128)
        return c

    lax.fori_loop(0, 8, rest, 0)
    store((update_ref, update_hbm), (gmid_ref, gmid_hbm))

    sum_scatter(sums, early_send, early_held, 4)


    widen(recv_d, 3)
    late_sums[...] = jnp.zeros_like(late_sums)

    sides = ((norm_l, inv_l, in_l, lw_ref, grads_l), (norm_r, inv_r, in_r, rw_ref, grads_r))

    def pre_grads(q, c):
        for side, (_, _, inputs, _, grads) in enumerate(sides):
            up = wide[pl.ds(side * 8 + q, N, stride=16), :]
            linear, switch = lin[side * 8 + q], sw[side * 8 + q]
            joined = jnp.concatenate(
                [up * switch, up * linear * switch * (1.0 - switch)], axis=0).astype(BF16)
            grads[q] = joined
            late_sums[side * 256:(side + 1) * 256, :] += dot(joined, inputs[q], 1, 0)
        return c

    lax.fori_loop(0, 8, pre_grads, 0)
    sum_scatter(late_sums, late_send, late_held, 7)
    sum_exchange(early_held, early_part, early_parts, 4)

    def back_step(q, c):
        outs = [
            rows_back(
                chunk(normed, q, side), chunk(inverse, q, side), dot(w_ref[...], grads[q], 1, 0).T)
            for side, (normed, inverse, _, w_ref, grads) in enumerate(sides)]
        for h in range(2):
            norm_l[pl.ds(q + 8 * h, 64, stride=16), :] = outs[0][h * 64:(h + 1) * 64]
        for h in range(4):
            norm_r[pl.ds(q + 8 * h, 32, stride=32), :] = outs[1][h * 32:(h + 1) * 32]
        return c

    lax.fori_loop(0, 8, back_step, 0)

    def round_step(t, c):
        at = rows_at(t * 128, 128, 128)
        gleft_ref[at, :] = norm_l[at, :].astype(BF16)
        gright_ref[at, :] = norm_r[at, :].astype(BF16)
        return c

    lax.fori_loop(0, 8, round_step, 0)
    store((gleft_ref, gleft_hbm), (gright_ref, gright_hbm))
    sum_exchange(late_held, late_part, late_parts, 7)
    sum_spread(early_parts, early_all, 4)
    sum_spread(late_parts, late_all, 7)
    sum_wait(early_all, 4)
    dgate_ref[...] = early_all[0:128, :].astype(F32)
    dout_ref[...] = early_all[128:256, :].astype(F32)
    sum_wait(late_all, 7)
    dleft_ref[...] = late_all[0:256, :].astype(F32).T
    dright_ref[...] = late_all[256:512, :].astype(F32).T
    store((dgate_ref, dgate_hbm), (dout_ref, dout_hbm), (dleft_ref, dleft_hbm), (dright_ref, dright_hbm))

    for k, send in enumerate((send_a, send_b, send_c, send_d)):
        most = send.at[pl.ds(0, N - 1)]
        copy(most, most, k, lax.rem(me + 1, N)).wait_send()
    sum_sent(early_all, early_parts, 4)
    sum_sent(late_all, late_parts, 7)
    for one in stores:
        one.wait()


def store_kernel(*refs):
    sources, targets, held, sems = refs[:8], refs[8:16], refs[16:24], refs[24]
    reads = [pltpu.make_async_copy(s, h, sems.at[n]) for n, (s, h) in enumerate(zip(sources, held))]
    writes = [pltpu.make_async_copy(h, t, sems.at[8 + n]) for n, (h, t) in enumerate(zip(held, targets))]
    for read in reads:
        read.start()
    for read, write in zip(reads, writes):
        read.wait()
        write.start()
    for write in writes:
        write.wait()


def per_device(left, right, middle, cotangent, lw, rw, gw, ow):
    tile = (N, 16, 128)
    pairs, flat, mids = (1024, 128), ((1024, 128), BF16), ((4, 16, 32, 128), BF16)
    results = [mids, flat, flat, mids] + [((128, 256), F32)] * 2 + [((128, 128), F32)] * 2
    shapes = [jax.ShapeDtypeStruct(s, t) for s, t in results]
    scratch = (
        results + [flat, flat, mids, mids] + [((128, 256), BF16)] * 2 + [((128, 128), BF16)] * 2
        + [((2048, 128), F32)] + [(tile, BF16)] * 8
        + [(pairs, F32)] * 4 + [((8, 128, 128), BF16)] * 2 + [((16, 128, 128), F32)] * 2
        + [((256, 128), BF16)] * 2 + [((16, 128, 128), F32)] * 2 + [((16, 128, 128), BF16)]
        + [((16, 128, 128), F32)] + [((16, 128, 128), BF16)] * 2
        + [((256, 512), BF16)] * 2 + [((512, 512), F32), ((512, 512), BF16)] + [((256, 128), F32), ((256, 512), F32)]
        + [((8, 256, 128), BF16)] * 2
        + [((256, 128), F32), ((512, 128), F32), ((256, 128), BF16), ((512, 128), BF16)]
        + [((16, 16, 128), BF16), ((16, 32, 128), BF16), ((16, 128), F32), ((32, 128), F32)]
        + [((8, 16, 128), F32), ((8, 32, 128), F32), ((256, 128), BF16), ((512, 128), BF16)]
    )
    outs = pl.pallas_call(
        kernel,
        out_shape=shapes,
        in_specs=[pl.BlockSpec(memory_space=pltpu.HBM)] * 8,
        out_specs=[pl.BlockSpec(memory_space=pltpu.HBM)] * 8,
        scratch_shapes=[pltpu.VMEM(s, t) for s, t in scratch] + [
            pltpu.SemaphoreType.DMA((20,)), pltpu.SemaphoreType.DMA((16,)), pltpu.SemaphoreType.DMA((8,)), pltpu.SemaphoreType.DMA((8,))],
        compiler_params=pltpu.CompilerParams(
            collective_id=0, has_side_effects=True, vmem_limit_bytes=61 * 2**20),
    )(
        left.reshape(pairs), right.reshape(pairs),
        middle.reshape(mids[0]), cotangent.reshape(mids[0]), lw, rw, gw, ow,
    )
    outs = pl.pallas_call(
        store_kernel,
        out_shape=shapes,
        in_specs=[pl.BlockSpec(memory_space=pltpu.HBM)] * 8,
        out_specs=[pl.BlockSpec(memory_space=pltpu.HBM)] * 8,
        scratch_shapes=[pltpu.VMEM(s, t) for s, t in results] + [pltpu.SemaphoreType.DMA((16,))],
        compiler_params=pltpu.CompilerParams(vmem_limit_bytes=61 * 2**20),
    )(*outs)
    return (
        outs[0].reshape(64, 32, 128), outs[1].reshape(64, 16, 128),
        outs[2].reshape(32, 32, 128), outs[3].reshape(64, 32, 128), *outs[4:],
    )


def solution(mesh):
    over_i = P(("rep", "rows"), "blk", None)
    over_j = P(("rep", "blk"), "rows", None)
    part = P("rep", None)
    return jax.shard_map(
        per_device,
        mesh=mesh,
        in_specs=(over_i, over_j, over_i, over_i, P(), P(), P(), P()),
        out_specs=(over_i, over_i, over_j, over_i, part, part, part, part),
        check_vma=False,
    )
```

time: 109 us -> 106 us (0.972)
  Pallas kernels: 108 us -> 105 us
    pallas_call x1, Pallas kernels: 106 us -> 102 us  [per_device(): pl.pallas_call(kernel, out_shape=shapes, in_specs=[pl.BlockSpec(memory_sp...]
where the time goes in v4:
time: 106 us; the launch traced here: 105 us
  Pallas kernels  105 us (99%)
    pallas_call x1, Pallas kernels, per_device(): pl.pallas_call(kernel, out_shape=shapes, in_specs=[pl.BlockSpec(memory_sp...  102 us
    pallas_call x1, Pallas kernels, per_device(): pl.pallas_call(store_kernel, out_shape=shapes, in_specs=[pl.BlockSpec(mem...  2.44 us

profile of v4, /device:TPU:2, one launch (start us, length us, event | category | flops | bytes accessed | tf_op | source)
XLA Modules:
  0.0 105.5 jit_solution(11141550061319241627)
XLA Ops:
  0.6 102.4 %shard_map.143 = (bf16[4,16,32,128]{3,2,1,0:T(8,128)(2,1)}, bf16[1024,128]{1,0:T(8,128)(2,1)}, bf16[1024,128]{1,0:T(8,128)(2,1)}, bf16[4,16,32,128]{3,2,1,0:T(8,...) custom-call(bf16[1024,128]{1,0:T(8,128)(2,1)} %bitcast.10, ...), custom_call_target="tpu_custom_call" | custom-call | tf_op jit(solution)/shard_map/pallas_call | solution.py:437
  103.0 2.4 %shard_map.144 = (bf16[4,16,32,128]{3,2,1,0:T(8,128)(2,1)}, bf16[1024,128]{1,0:T(8,128)(2,1)}, bf16[1024,128]{1,0:T(8,128)(2,1)}, bf16[4,16,32,128]{3,2,1,0:T(8,...) custom-call(bf16[4,16,32,128]{3,2,1,0:T(8,128)(2,1)} %get-tuple-element.24.refs_0_, ...), custom_call_target="tpu_custom_call" | custom-call | tf_op jit(solution)/shard_map/pallas_call | solution.py:450

commit v5 on v4

--- a/solution.py
+++ b/solution.py
@@ -64,7 +64,7 @@
     norm_l, norm_r, inv_l, inv_r, in_l, in_r, lin, sw,
     lwt, rwt, mid_norm, mid_inv, mid_t, gate, head_back, tri_in,
     lt, rt, tri, tb, lb, rb,
-    grads_l, grads_r, sums, late_sums, early_send, late_send, early_held, late_held,
+    grads_l, grads_r, sums, late_sums, early_send, early_held, late_held,
     early_part, late_part, early_parts, late_parts, early_all, late_all, sems, arrive_sems, fetch_sems, store_sems,
 ):
     my_row, my_blk = lax.axis_index("rows"), lax.axis_index("blk")
@@ -118,15 +118,17 @@
         copy(recv.at[part], recv.at[part], k, lax.rem(me + 1, N), arrive_sems.at[4 * k + g]).wait_recv()
         return pair(g)[1]
 
+    def widen_part(recv, h):
+        def step(t, c):
+            at = h * 32 + t * 16
+            wide[rows_at(at * 16, 256, 256), :] = (
+                recv[rows_at(at, 16, 16)].astype(F32).reshape(256, 128))
+            return c
+        lax.fori_loop(0, 2, step, 0)
+
     def widen(recv, k):
         for g in range(4):
-            first = arrived(recv, k, g) * 32
-            def step(t, c):
-                at = first + t * 16
-                wide[rows_at(at * 16, 256, 256), :] = (
-                    recv[rows_at(at, 16, 16)].astype(F32).reshape(256, 128))
-                return c
-            lax.fori_loop(0, 2, step, 0)
+            widen_part(recv, arrived(recv, k, g))
 
     for fetch in fetches[:4]:
         fetch.wait()
@@ -254,8 +256,11 @@
         held[my_blk] = send[rows_at(my_blk * rows, rows, rows), :]
 
     def sum_exchange(held, part, parts, k):
-        copy(held.at[pl.ds(0, 15)], held.at[pl.ds(0, 15)], k, over_blk(1)).wait_recv()
-        part[...] = jnp.sum(held[...].astype(F32), axis=0)
+        slots = held.shape[0] // 16
+        most = held.at[pl.ds(0, 15 * slots)]
+        copy(most, most, k, over_blk(1)).wait_recv()
+        part[...] = jnp.concatenate(
+            [jnp.sum(held[16 * n:16 * n + 16].astype(F32), axis=0) for n in range(slots)], axis=0)
         for o in range(1, 8):
             copy(part, parts.at[my_row], k + 1, lax.rem(me + 16 * o, N)).start()
         parts[my_row] = part[...]
@@ -272,9 +277,10 @@
         most = pl.ds(0, whole.shape[0] // 16 * 15)
         copy(whole.at[most], whole.at[most], k + 2, over_blk(1)).wait_recv()
 
-    def sum_sent(whole, parts, k):
+    def sum_sent(held, whole, parts, k):
+        most = held.at[pl.ds(0, held.shape[0] // 16 * 15)]
+        copy(most, most, k, over_blk(1)).wait_send()
         most = pl.ds(0, whole.shape[0] // 16 * 15)
-        copy(whole.at[most], whole.at[most], k, over_blk(1)).wait_send()
         copy(parts.at[pl.ds(0, 7)], parts.at[pl.ds(0, 7)], k + 1, over_blk(1)).wait_send()
         copy(whole.at[most], whole.at[most], k + 2, over_blk(1)).wait_send()
 
@@ -344,23 +350,30 @@
     sum_scatter(sums, early_send, early_held, 4)
 
 
-    widen(recv_d, 3)
-    late_sums[...] = jnp.zeros_like(late_sums)
-
     sides = ((norm_l, inv_l, in_l, lw_ref, grads_l), (norm_r, inv_r, in_r, rw_ref, grads_r))
-
-    def pre_grads(q, c):
+    for g in range(4):
+        h = arrived(recv_d, 3, g)
+        widen_part(recv_d, h)
+        low = rows_at(h * 32, 32, 32)
+        high = rows_at(h * 32 + 128, 32, 32)
         for side, (_, _, inputs, _, grads) in enumerate(sides):
-            up = wide[pl.ds(side * 8 + q, N, stride=16), :]
-            linear, switch = lin[side * 8 + q], sw[side * 8 + q]
+            ups, switches = [], []
+            for q in range(8):
+                up = wide[pl.ds(h * 512 + side * 8 + q, 32, stride=16), :]
+                linear, switch = lin[side * 8 + q, low, :], sw[side * 8 + q, low, :]
+                ups.append((up * switch).astype(BF16))
+                switches.append((up * linear * switch * (1.0 - switch)).astype(BF16))
+                grads[q, low, :] = ups[q]
+                grads[q, high, :] = switches[q]
             joined = jnp.concatenate(
-                [up * switch, up * linear * switch * (1.0 - switch)], axis=0).astype(BF16)
-            grads[q] = joined
-            late_sums[side * 256:(side + 1) * 256, :] += dot(joined, inputs[q], 1, 0)
-        return c
-
-    lax.fori_loop(0, 8, pre_grads, 0)
-    sum_scatter(late_sums, late_send, late_held, 7)
+                [jnp.concatenate(ups, axis=1), jnp.concatenate(switches, axis=1)], axis=0)
+            late_sums[rows_at(h * 128 + side * 64, 64, 64), :] = dot(
+                joined, inputs[...].reshape(1024, 128), 1, 0)
+        for o in range(1, 16):
+            p = over_blk(o)
+            piece = rows_at(h * 128 + lax.rem(p, 16) * 8, 8, 8)
+            copy(late_sums.at[piece], late_held.at[h * 16 + my_blk], 7, p).start()
+        late_held[h * 16 + my_blk] = late_sums[rows_at(h * 128 + my_blk * 8, 8, 8), :]
     sum_exchange(early_held, early_part, early_parts, 4)
 
     def back_step(q, c):
@@ -391,15 +404,19 @@
     dgate_ref[...] = early_all[0:128, :].astype(F32)
     dout_ref[...] = early_all[128:256, :].astype(F32)
     sum_wait(late_all, 7)
-    dleft_ref[...] = late_all[0:256, :].astype(F32).T
-    dright_ref[...] = late_all[256:512, :].astype(F32).T
+    whole = late_all[...].astype(F32)
+    for side, target in enumerate((dleft_ref, dright_ref)):
+        target[...] = jnp.concatenate([
+            whole[b * 32 + h * 8:b * 32 + h * 8 + 8]
+            for kind in range(2) for h in range(4)
+            for b in range(side * 8 + kind * 4, side * 8 + kind * 4 + 4)], axis=0).T
     store((dgate_ref, dgate_hbm), (dout_ref, dout_hbm), (dleft_ref, dleft_hbm), (dright_ref, dright_hbm))
 
     for k, send in enumerate((send_a, send_b, send_c, send_d)):
         most = send.at[pl.ds(0, N - 1)]
         copy(most, most, k, lax.rem(me + 1, N)).wait_send()
-    sum_sent(early_all, early_parts, 4)
-    sum_sent(late_all, late_parts, 7)
+    sum_sent(early_held, early_all, early_parts, 4)
+    sum_sent(late_held, late_all, late_parts, 7)
     for one in stores:
         one.wait()
 
@@ -430,8 +447,8 @@
         + [((16, 128, 128), F32)] + [((16, 128, 128), BF16)] * 2
         + [((256, 512), BF16)] * 2 + [((512, 512), F32), ((512, 512), BF16)] + [((256, 128), F32), ((256, 512), F32)]
         + [((8, 256, 128), BF16)] * 2
-        + [((256, 128), F32), ((512, 128), F32), ((256, 128), BF16), ((512, 128), BF16)]
-        + [((16, 16, 128), BF16), ((16, 32, 128), BF16), ((16, 128), F32), ((32, 128), F32)]
+        + [((256, 128), F32), ((512, 128), F32), ((256, 128), BF16)]
+        + [((16, 16, 128), BF16), ((64, 8, 128), F32), ((16, 128), F32), ((32, 128), F32)]
         + [((8, 16, 128), F32), ((8, 32, 128), F32), ((256, 128), BF16), ((512, 128), BF16)]
     )
     outs = pl.pallas_call(

time: 106 us -> 105 us (level)
  no operation moved by 1% of the time
where the time goes in v5:
time: 105 us
  Pallas kernels  104 us (99%)
    pallas_call x1, Pallas kernels, per_device(): pl.pallas_call(kernel, out_shape=shapes, in_specs=[pl.BlockSpec(memory_sp...  102 us
    pallas_call x1, Pallas kernels, per_device(): pl.pallas_call(store_kernel, out_shape=shapes, in_specs=[pl.BlockSpec(mem...  2.44 us

profile of v5, /device:TPU:2, one launch (start us, length us, event | category | flops | bytes accessed | tf_op | source)
XLA Modules:
  0.0 104.7 jit_solution(16128026914305131411)
XLA Ops:
  0.6 101.6 %shard_map.143 = (bf16[4,16,32,128]{3,2,1,0:T(8,128)(2,1)}, bf16[1024,128]{1,0:T(8,128)(2,1)}, bf16[1024,128]{1,0:T(8,128)(2,1)}, bf16[4,16,32,128]{3,2,1,0:T(8,...) custom-call(bf16[1024,128]{1,0:T(8,128)(2,1)} %bitcast.10, ...), custom_call_target="tpu_custom_call" | custom-call | tf_op jit(solution)/shard_map/pallas_call | solution.py:454
  102.2 2.4 %shard_map.144 = (bf16[4,16,32,128]{3,2,1,0:T(8,128)(2,1)}, bf16[1024,128]{1,0:T(8,128)(2,1)}, bf16[1024,128]{1,0:T(8,128)(2,1)}, bf16[4,16,32,128]{3,2,1,0:T(8,...) custom-call(bf16[4,16,32,128]{3,2,1,0:T(8,128)(2,1)} %get-tuple-element.24.refs_0_, ...), custom_call_target="tpu_custom_call" | custom-call | tf_op jit(solution)/shard_map/pallas_call | solution.py:467

commit v6 on v5

--- a/solution.py
+++ b/solution.py
@@ -243,86 +243,6 @@
     lax.fori_loop(0, 8, heads, 0)
     spread(send_c, recv_c, 2)
 
-    def over_blk(o):
-        return my_row * 16 + lax.rem(my_blk + o, 16)
-
-    def sum_scatter(src, send, held, k):
-        send[...] = src[...].astype(BF16)
-        rows = held.shape[1]
-        for o in range(1, 16):
-            p = over_blk(o)
-            at = rows_at(lax.rem(p, 16) * rows, rows, rows)
-            copy(send.at[at], held.at[my_blk], k, p).start()
-        held[my_blk] = send[rows_at(my_blk * rows, rows, rows), :]
-
-    def sum_exchange(held, part, parts, k):
-        slots = held.shape[0] // 16
-        most = held.at[pl.ds(0, 15 * slots)]
-        copy(most, most, k, over_blk(1)).wait_recv()
-        part[...] = jnp.concatenate(
-            [jnp.sum(held[16 * n:16 * n + 16].astype(F32), axis=0) for n in range(slots)], axis=0)
-        for o in range(1, 8):
-            copy(part, parts.at[my_row], k + 1, lax.rem(me + 16 * o, N)).start()
-        parts[my_row] = part[...]
-
-    def sum_spread(parts, whole, k):
-        copy(parts.at[pl.ds(0, 7)], parts.at[pl.ds(0, 7)], k + 1, lax.rem(me + 16, N)).wait_recv()
-        rows = parts.shape[1]
-        at = rows_at(my_blk * rows, rows, rows)
-        whole[at, :] = jnp.sum(parts[...], axis=0).astype(BF16)
-        for o in range(1, 16):
-            copy(whole.at[at], whole.at[at], k + 2, over_blk(o)).start()
-
-    def sum_wait(whole, k):
-        most = pl.ds(0, whole.shape[0] // 16 * 15)
-        copy(whole.at[most], whole.at[most], k + 2, over_blk(1)).wait_recv()
-
-    def sum_sent(held, whole, parts, k):
-        most = held.at[pl.ds(0, held.shape[0] // 16 * 15)]
-        copy(most, most, k, over_blk(1)).wait_send()
-        most = pl.ds(0, whole.shape[0] // 16 * 15)
-        copy(parts.at[pl.ds(0, 7)], parts.at[pl.ds(0, 7)], k + 1, over_blk(1)).wait_send()
-        copy(whole.at[most], whole.at[most], k + 2, over_blk(1)).wait_send()
-
-    for g in range(4):
-        h = arrived(recv_c, 2, g)
-        at = rows_at(h * 128, 128, 128)
-
-        def unpack_tb(n, c):
-            r = h * 2 + n
-            tiles = [recv_c[r * 16 + t].astype(F32) for t in range(16)]
-            outs = [jnp.concatenate(swap4(tiles[4 * v:4 * v + 4]), axis=0) for v in range(4)]
-            tb[rows_at(r * 64, 64, 64), :] = jnp.concatenate(outs, axis=1).astype(BF16)
-            return c
-
-        lax.fori_loop(0, 2, unpack_tb, 0)
-        lb[...] = dot(rt[...], tb[at, :], 1, 1)
-        if g == 0:
-            rb[...] = dot(lt[:, at], tb[at, :], 1, 0)
-        else:
-            rb[...] += dot(lt[:, at], tb[at, :], 1, 0)
-
-        def pack_left(n, c):
-            tiles = [lb[rows_at((n * 4 + u) * 16, 16, 16), :] for u in range(4)]
-            outs = [swap2(tile[:8], tile[8:]) for tile in tiles]
-            for u in range(4):
-                for v in range(2):
-                    wide[rows_at((h * 32 + 16 * v + n * 4 + u) * 16, 8, 8), :] = outs[u][v]
-            return c
-
-        lax.fori_loop(0, 4, pack_left, 0)
-
-    def pack_right(r, c):
-        rows = rb[rows_at(r * 32, 32, 32), :]
-        outs = [swap4([rows[8 * v:8 * v + 8, g * 128:(g + 1) * 128] for v in range(4)]) for g in range(4)]
-        for g in range(4):
-            for t in range(4):
-                wide[rows_at((r * 16 + 4 * g + t) * 16 + 8, 8, 8), :] = outs[g][t]
-        return c
-
-    lax.fori_loop(0, 8, pack_right, 0)
-    spread(send_d, recv_d, 3)
-
     sums[...] = jnp.zeros_like(sums)
 
     def rest(q, c):
@@ -344,7 +264,89 @@
             gmid_ref[:, s] = out.reshape(4, 32, 128)
         return c
 
-    lax.fori_loop(0, 8, rest, 0)
+    lax.fori_loop(0, 3, rest, 0)
+
+    def over_blk(o):
+        return my_row * 16 + lax.rem(my_blk + o, 16)
+
+    def sum_scatter(src, send, held, k):
+        send[...] = src[...].astype(BF16)
+        rows = held.shape[1]
+        for o in range(1, 16):
+            p = over_blk(o)
+            at = rows_at(lax.rem(p, 16) * rows, rows, rows)
+            copy(send.at[at], held.at[my_blk], k, p).start()
+        held[my_blk] = send[rows_at(my_blk * rows, rows, rows), :]
+
+    def sum_exchange(held, part, parts, k):
+        slots = held.shape[0] // 16
+        most = held.at[pl.ds(0, 15 * slots)]
+        copy(most, most, k, over_blk(1)).wait_recv()
+        part[...] = jnp.concatenate(
+            [jnp.sum(held[16 * n:16 * n + 16].astype(F32), axis=0) for n in range(slots)], axis=0)
+        for o in range(1, 8):
+            copy(part, parts.at[my_row], k + 1, lax.rem(me + 16 * o, N)).start()
+        parts[my_row] = part[...]
+
+    def sum_spread(parts, whole, k):
+        copy(parts.at[pl.ds(0, 7)], parts.at[pl.ds(0, 7)], k + 1, lax.rem(me + 16, N)).wait_recv()
+        rows = parts.shape[1]
+        at = rows_at(my_blk * rows, rows, rows)
+        whole[at, :] = jnp.sum(parts[...], axis=0).astype(BF16)
+        for o in range(1, 16):
+            copy(whole.at[at], whole.at[at], k + 2, over_blk(o)).start()
+
+    def sum_wait(whole, k):
+        most = pl.ds(0, whole.shape[0] // 16 * 15)
+        copy(whole.at[most], whole.at[most], k + 2, over_blk(1)).wait_recv()
+
+    def sum_sent(held, whole, parts, k):
+        most = held.at[pl.ds(0, held.shape[0] // 16 * 15)]
+        copy(most, most, k, over_blk(1)).wait_send()
+        most = pl.ds(0, whole.shape[0] // 16 * 15)
+        copy(parts.at[pl.ds(0, 7)], parts.at[pl.ds(0, 7)], k + 1, over_blk(1)).wait_send()
+        copy(whole.at[most], whole.at[most], k + 2, over_blk(1)).wait_send()
+
+    for g in range(4):
+        h = arrived(recv_c, 2, g)
+        at = rows_at(h * 128, 128, 128)
+
+        def unpack_tb(n, c):
+            r = h * 2 + n
+            tiles = [recv_c[r * 16 + t].astype(F32) for t in range(16)]
+            outs = [jnp.concatenate(swap4(tiles[4 * v:4 * v + 4]), axis=0) for v in range(4)]
+            tb[rows_at(r * 64, 64, 64), :] = jnp.concatenate(outs, axis=1).astype(BF16)
+            return c
+
+        lax.fori_loop(0, 2, unpack_tb, 0)
+        lb[...] = dot(rt[...], tb[at, :], 1, 1)
+        if g == 0:
+            rb[...] = dot(lt[:, at], tb[at, :], 1, 0)
+        else:
+            rb[...] += dot(lt[:, at], tb[at, :], 1, 0)
+
+        def pack_left(n, c):
+            tiles = [lb[rows_at((n * 4 + u) * 16, 16, 16), :] for u in range(4)]
+            outs = [swap2(tile[:8], tile[8:]) for tile in tiles]
+            for u in range(4):
+                for v in range(2):
+                    wide[rows_at((h * 32 + 16 * v + n * 4 + u) * 16, 8, 8), :] = outs[u][v]
+            return c
+
+        lax.fori_loop(0, 4, pack_left, 0)
+
+    def pack_right(r, c):
+        rows = rb[rows_at(r * 32, 32, 32), :]
+        outs = [swap4([rows[8 * v:8 * v + 8, g * 128:(g + 1) * 128] for v in range(4)]) for g in range(4)]
+        for g in range(4):
+            for t in range(4):
+                wide[rows_at((r * 16 + 4 * g + t) * 16 + 8, 8, 8), :] = outs[g][t]
+        return c
+
+    lax.fori_loop(0, 8, pack_right, 0)
+    spread(send_d, recv_d, 3)
+
+    lax.fori_loop(3, 8, rest, 0)
     store((update_ref, update_hbm), (gmid_ref, gmid_hbm))
 
     sum_scatter(sums, early_send, early_held, 4)

time: 105 us -> 105 us (level)
  no operation moved by 1% of the time
where the time goes in v6:
time: 105 us
  Pallas kernels  104 us (99%)
    pallas_call x1, Pallas kernels, per_device(): pl.pallas_call(kernel, out_shape=shapes, in_specs=[pl.BlockSpec(memory_sp...  102 us
    pallas_call x1, Pallas kernels, per_device(): pl.pallas_call(store_kernel, out_shape=shapes, in_specs=[pl.BlockSpec(mem...  2.44 us

profile of v6, /device:TPU:2, one launch (start us, length us, event | category | flops | bytes accessed | tf_op | source)
XLA Modules:
  0.0 104.7 jit_solution(2767109674968998377)
XLA Ops:
  0.6 101.6 %shard_map.143 = (bf16[4,16,32,128]{3,2,1,0:T(8,128)(2,1)}, bf16[1024,128]{1,0:T(8,128)(2,1)}, bf16[1024,128]{1,0:T(8,128)(2,1)}, bf16[4,16,32,128]{3,2,1,0:T(8,...) custom-call(bf16[1024,128]{1,0:T(8,128)(2,1)} %bitcast.10, ...), custom_call_target="tpu_custom_call" | custom-call | tf_op jit(solution)/shard_map/pallas_call | solution.py:456
  102.2 2.4 %shard_map.144 = (bf16[4,16,32,128]{3,2,1,0:T(8,128)(2,1)}, bf16[1024,128]{1,0:T(8,128)(2,1)}, bf16[1024,128]{1,0:T(8,128)(2,1)}, bf16[4,16,32,128]{3,2,1,0:T(8,...) custom-call(bf16[4,16,32,128]{3,2,1,0:T(8,128)(2,1)} %get-tuple-element.24.refs_0_, ...), custom_call_target="tpu_custom_call" | custom-call | tf_op jit(solution)/shard_map/pallas_call | solution.py:469
